TPU v7x, 32 devices: a whole 2x2x4 slice. The times are simulated.
32 devices in a mesh: group: 2 (over y), expert: 4 (over x, core), replica: 4 (over z).
Axes of the slice: x: 2, y: 2, z: 4, core: 2. Of those that a mesh axis runs over, the one named last changes fastest.
Arguments:
- tokens: bfloat16 [1024, 7168], P(('group', 'expert')), parts along dimension 0, may hold values from -6 to 6
- route_ids: int32 [1024, 8], P(('group', 'expert')), parts along dimension 0, may hold values from 0 to 255, all different within a row
- route_gates: float32 [1024, 8], P(('group', 'expert')), parts along dimension 0, may hold values from 0.2 to 1
- copy_source: int32 [8], P('group'), parts along dimension 0, may hold values from 0 to 3, each once
- copy_share: int32 [8], P('group'), parts along dimension 0, may hold values from 0 to 128, as said below
- w_gate_up: bfloat16 [4, 7168, 2, 1024], P('expert', None, None, 'replica'), may hold values from -0.0625 to 0.0625
- w_down: bfloat16 [4, 1024, 7168], P('expert', 'replica'), may hold values from -0.1875 to 0.1875
- shared_gate_up: bfloat16 [7168, 2, 1024], P(None, None, 'replica'), may hold values from -0.0625 to 0.0625
- shared_down: bfloat16 [1024, 7168], P('replica'), may hold values from -0.1875 to 0.1875
Outputs:
- mixed: bfloat16 [1024, 7168], P(('group', 'expert', 'replica')), parts along dimension 0
There are 2 independent parts, one for each index of `group`. A program takes and returns all parts, laid end to end along the dimension named above; an argument that names none is the same for every part. Nothing has to cross between parts.
Inputs may be any that keep to these rules, and one draw needn't show every extreme that they name: `copy_source`: every expert of the layer appears exactly once. `copy_share`: some expert has 0 and another has 128. `route_ids`: the 8 experts of a token are distinct.
All inputs are finite; a program needn't handle non-finite values.
Results may differ from a plain program's by a relative error of at most 0.0051.
Values may be sent and summed in bfloat16 or wider, within the bound.
No kernel may reach another device: no remote copies, remote signals or barrier semaphores. Data moves between devices by JAX's collectives and lax.ppermute only.
A program may use at most 128 MiB of HBM per device.

v0:
```python
import jax
import jax.numpy as jnp
from jax import lax
from jax.sharding import PartitionSpec as P


def plan_block(route_rows, copy_source, copy_share, experts, capacity):
    row_count, top_count = route_rows.shape
    inside = route_rows < experts
    expert = jnp.where(inside, route_rows, 0)
    holders = jnp.arange(experts, dtype=jnp.int32)
    flattened = expert.reshape(-1)
    matches = flattened[:, None] == holders[None, :]
    share_limit = jnp.sum(jnp.where(matches, copy_share[None, :], 0), axis=1).reshape(
        row_count, top_count
    )
    new_home = jnp.sum(
        jnp.where(copy_source[None, :] == flattened[:, None], holders[None, :], 0), axis=1
    ).reshape(row_count, top_count)
    position = jnp.arange(row_count, dtype=jnp.int32)[:, None]
    by_copy = inside & (position < share_limit)
    holder = jnp.where(by_copy, new_home, expert)
    member = (
        (holder.reshape(-1)[:, None] == holders[None, :]) & inside.reshape(-1)[:, None]
    ).astype(jnp.int32)
    before = jnp.cumsum(member, axis=0) - member
    rank_index = jnp.sum(before * member, axis=1).reshape(row_count, top_count)
    served = inside & (rank_index < capacity)
    return (expert, by_copy, holder, rank_index, served)


def swiglu(row_block, weights, half_width):
    projected = jnp.dot(row_block, weights, preferred_element_type=jnp.float32)
    return (jax.nn.silu(projected[:, :half_width]) * projected[:, half_width:]).astype(jnp.bfloat16)


def shards(
    tokens,
    route_ids,
    route_gates,
    copy_source,
    copy_share,
    w_gate_up,
    w_down,
    shared_gate_up,
    shared_down,
):
    expert_count = lax.axis_size("expert")
    replica_count = lax.axis_size("replica")
    tok_rows, model_width = tokens.shape
    top_count = route_ids.shape[1]
    slice_width = w_down.shape[1]
    capacity = max(2, tok_rows * 3 // 64)
    expert, by_copy, holder, rank_index, served = plan_block(
        route_ids, copy_source, copy_share, expert_count, capacity
    )
    resident_up = w_gate_up.reshape(model_width, 2 * slice_width)
    resident_down = w_down.reshape(slice_width, model_width)
    slot_count = 2 * capacity
    slot_index = rank_index + capacity * by_copy.astype(jnp.int32)
    table_size = expert_count * slot_count
    position = jnp.where(served, expert * slot_count + slot_index, table_size).reshape(-1)
    slot_ids = jnp.arange(table_size, dtype=jnp.int32)
    matches = position[None, :] == slot_ids[:, None]
    route_order = jnp.arange(position.shape[0], dtype=jnp.int32)
    source = jnp.sum(jnp.where(matches, route_order[None, :], 0), axis=1)
    filled = jnp.any(matches, axis=1)
    token_of = source // top_count
    gate_of = jnp.where(filled, route_gates.reshape(-1)[source], 0.0)
    outgoing = tokens[token_of].reshape(expert_count, slot_count, model_width)
    received = lax.all_to_all(outgoing, "expert", split_axis=0, concat_axis=0, tiled=True)
    flattened = received.reshape(-1, model_width)
    hidden = swiglu(flattened, resident_up, slice_width)
    results = jnp.dot(hidden, resident_down, preferred_element_type=jnp.float32).astype(
        jnp.bfloat16
    )
    answers = lax.all_to_all(
        results.reshape(received.shape), "expert", split_axis=0, concat_axis=0, tiled=True
    )
    weighted = answers.reshape(table_size, model_width).astype(jnp.float32) * gate_of[:, None]
    shared_width = shared_down.shape[0]
    shared_up = shared_gate_up.reshape(model_width, 2 * shared_width)
    hidden = swiglu(tokens, shared_up, shared_width)
    result = jnp.dot(hidden, shared_down, preferred_element_type=jnp.float32)
    row_ids = jnp.arange(tok_rows // replica_count * lax.axis_size("replica"), dtype=jnp.int32)
    selector = ((token_of[None, :] == row_ids[:, None]) & filled[None, :]).astype(jnp.float32)
    mixed = lax.psum_scatter(
        result + jnp.dot(selector, weighted, precision=lax.Precision.HIGHEST),
        "replica",
        scatter_dimension=0,
        tiled=True,
    )
    return mixed.astype(jnp.bfloat16)


def solution(mesh):
    return jax.shard_map(
        shards,
        mesh=mesh,
        in_specs=(
            P(("group", "expert"), None),
            P(("group", "expert"), None),
            P(("group", "expert"), None),
            P("group"),
            P("group"),
            P("expert", None, None, "replica"),
            P("expert", "replica", None),
            P(None, None, "replica"),
            P("replica", None),
        ),
        out_specs=P(("group", "expert", "replica"), None),
        check_vma=False,
    )
```

profile of v0, /device:TPU:0, one launch (start us, length us, event | category | flops | bytes accessed | tf_op | source)
XLA Modules:
  0.0 147.3 jit_solution(15698150540257320992)
XLA Ops:
  6.5 0.0 copy-start
  6.5 0.9 copy.13
  7.5 0.1 and.65
  7.6 0.1 and.62
  7.7 0.1 eq.81
  7.8 0.8 select_reduce_fusion.1
  8.5 0.1 reshape.153
  8.6 0.1 reshape.152
  8.8 0.1 eq.92
  8.8 0.1 eq.88
  9.0 1.1 reduce-window.6
  10.1 0.2 slice_reduce_fusion
  10.3 0.2 reduce-window.9
  10.5 0.1 add_bitcast_fusion
  10.6 0.1 reshape.155
  10.7 0.1 eq.96
  10.8 0.1 select_reduce_fusion
  11.0 0.0 copy-done
  11.0 0.0 copy-start.3
  11.0 1.0 gather_fusion
  12.0 1.1 reshape.156
  13.1 4.2 %all-to-all-start = ((bf16[4,12,7168]{2,1,0:T(8,128)(2,1)}), bf16[4,12,7168]{2,1,0:T(8,128)(2,1)S(1)}, u32[]{:S(2)}, u32[]{:S(2)}) async-start(bf16[4,12,7168]{2,1,0:T(8,128)(2,1)} %reshape.156), calls=%async_computation | async-start | bytes 1835008 | tf_op jit(solution)/shard_map/all_to_all | solution.py:71
  17.3 0.1 fusion.3
  17.4 0.0 copy-done.3
  17.4 0.1 copy.15
  17.5 0.1 reshape.161
  17.6 7.3 %copy.18 = bf16[896,8,2,256]{3,1,2,0:T(8,128)(2,1)} copy(bf16[896,8,2,256]{3,2,1,0:T(2,128)(2,1)} %bitcast.49) | data formatting | bytes 14680064
  25.0 7.4 %copy.16 = bf16[896,8,2,256]{3,1,2,0:T(8,128)(2,1)} copy(bf16[896,8,2,256]{3,2,1,0:T(2,128)(2,1)} %bitcast.50) | data formatting | bytes 14680064
  32.4 0.7 gather_fusion.1
  33.1 4.9 %fusion.28 = f32[128,512]{1,0:T(8,128)} fusion(bf16[128,7168]{1,0:T(8,128)(2,1)S(1)} %copy-done, bf16[7168,512]{1,0:T(8,128)(2,1)} %bitcast.47), kind=kOutput, calls=%fused_computation.59 | convolution fusion | flops 939524096 | bytes 9437184 | tf_op jit(solution)/shard_map/dot_general | solution.py:33
  38.0 0.0 all-to-all-done
  38.0 0.2 reshape.157
  38.2 0.0 copy-start.1
  38.2 4.6 %fusion.29 = f32[48,512]{1,0:T(8,128)S(1)} fusion(bf16[48,7168]{1,0:T(8,128)(2,1)S(1)} %reshape.157, bf16[7168,512]{1,0:T(8,128)(2,1)} %bitcast.48), kind=kOutput, calls=%fused_computation.60 | convolution fusion | flops 352321536 | bytes 8126464 | tf_op jit(solution)/shard_map/dot_general | solution.py:33
  42.8 0.0 copy-done.1
  42.8 0.0 copy-start.2
  42.8 0.7 convolution_convert_fusion
  43.5 1.1 reshape.160
  44.6 4.2 %all-to-all-start.1 = ((bf16[4,12,7168]{2,1,0:T(8,128)(2,1)}), bf16[4,12,7168]{2,1,0:T(8,128)(2,1)}, u32[]{:S(2)}, u32[]{:S(2)}) async-start(bf16[4,12,7168]{2,1,0:T(8,128)(2,1)} %reshape.160), calls=%async_computation.1 | async-start | bytes 1835008 | tf_op jit(solution)/shard_map/all_to_all | solution.py:77
  48.9 0.0 reduce-scatter.2.cloned.1.call-start
  48.9 0.0 copy-done.2
  48.9 4.5 %fusion.5 = f32[128,7168]{1,0:T(8,128)} fusion(bf16[256,7168]{1,0:T(8,128)(2,1)} %param.17, f32[128,512]{1,0:T(8,128)S(1)} %copy-done.2), kind=kOutput, calls=%fused_computation.12 | convolution fusion | flops 469958656 | bytes 7602176 | tf_op jit(solution)/shard_map/dot_general | solution.py:84
  53.5 8.5 %all-to-all-done.1 = bf16[4,12,7168]{2,1,0:T(8,128)(2,1)} async-done(((bf16[4,12,7168]{2,1,0:T(8,128)(2,1)}), bf16[4,12,7168]{2,1,0:T(8,128)(2,1)}, u32[]{:S(2)}, u32[]{:S(2)}) %all-to-all-start.1) | async-done | bytes 688160 | tf_op jit(solution)/shard_map/all_to_all | solution.py:77
  62.0 1.3 reshape.162
  63.3 5.5 %convolution_add_fusion = f32[128,7168]{1,0:T(8,128)} fusion(f32[128,7168]{1,0:T(8,128)} %fusion.5, f32[48,7168]{1,0:T(8,128)S(1)} %reshape.162, f32[48]{0:T(128)S(1)} %broadcast_select_fusion.1, s32[48]{0:T(128)S(1)} %and_select_fusion.1, pred[48]{0:T(512)(128)(4,1)S(1)} %fusion.3), kind=kOutput, calls=%fused_computation.2 | convolution fusion | flops 529756160 | bytes 8716720 | tf_op jit(solution)/shard_map/dot_general | solution.py:88
  68.9 0.0 reduce-scatter.2.cloned.1.call-update
  68.9 69.6 %reduce-scatter.2.cloned.1.call-done = f32[32,7168]{1,0:T(8,128)} async-done(((f32[128,7168]{1,0:T(8,128)}), f32[32,7168]{1,0:T(8,128)}) %reduce-scatter.2.cloned.1.call-update) | async-done | bytes 917520 | tf_op jit(solution)/shard_map/reduce_scatter | solution.py:87
  138.5 2.0 %convert_element_type.34 = bf16[32,7168]{1,0:T(8,128)(2,1)} convert(f32[32,7168]{1,0:T(8,128)} %reduce-scatter.2.cloned.1.call-done) | non-fusion elementwise | flops 229376 | bytes 1376256 | tf_op jit(solution)/shard_map/convert_element_type | solution.py:93
  (9 shorter events, 0.1 us)
Async XLA Ops:
  6.5 4.5 %copy-start = (bf16[128,7168]{1,0:T(8,128)(2,1)S(1)}, bf16[128,7168]{1,0:T(8,128)(2,1)}, u32[]{:S(2)}) copy-start(bf16[128,7168]{1,0:T(8,128)(2,1)} %param.9) | copy-start | bytes 5505028
  11.0 6.4 %copy-start.3 = (f32[128,8]{0,1:T(8,128)S(1)}, f32[128,8]{0,1:T(8,128)}, u32[]{:S(2)}) copy-start(f32[128,8]{0,1:T(8,128)} %param.11) | copy-start | bytes 12292
  13.1 24.9 %all-to-all-start = ((bf16[4,12,7168]{2,1,0:T(8,128)(2,1)}), bf16[4,12,7168]{2,1,0:T(8,128)(2,1)S(1)}, u32[]{:S(2)}, u32[]{:S(2)}) async-start(bf16[4,12,7168]{2,1,0:T(8,128)(2,1)} %reshape.156), calls=%async_computation | async-start | bytes 1835008 | tf_op jit(solution)/shard_map/all_to_all | solution.py:71
  38.2 4.6 %copy-start.1 = (bf16[1,256,7168]{2,1,0:T(8,128)(2,1)S(1)}, bf16[1,256,7168]{2,1,0:T(8,128)(2,1)}, u32[]{:S(2)}) copy-start(bf16[1,256,7168]{2,1,0:T(8,128)(2,1)} %param.15) | copy-start | bytes 11010052
  42.8 6.1 %copy-start.2 = (f32[128,512]{1,0:T(8,128)S(1)}, f32[128,512]{1,0:T(8,128)}, u32[]{:S(2)}) copy-start(f32[128,512]{1,0:T(8,128)} %fusion.28) | copy-start | bytes 786436
  44.6 17.4 %all-to-all-start.1 = ((bf16[4,12,7168]{2,1,0:T(8,128)(2,1)}), bf16[4,12,7168]{2,1,0:T(8,128)(2,1)}, u32[]{:S(2)}, u32[]{:S(2)}) async-start(bf16[4,12,7168]{2,1,0:T(8,128)(2,1)} %reshape.160), calls=%async_computation.1 | async-start | bytes 1835008 | tf_op jit(solution)/shard_map/all_to_all | solution.py:77
  48.9 89.6 %reduce-scatter.2.cloned.1.call-start = ((), (), s32[]{:S(2)}) async-start(), calls=%async_computation.3 | async-start | bytes 4587520 | tf_op jit(solution)/shard_map/reduce_scatter | solution.py:87
Sparse Core Ops, SparseCore 0:
  69.0 69.4 reduce-scatter.1
where the time goes:
time: 148 us; the launch traced here: 147 us
  waiting for transfers between devices  78.2 us (53%)
  local copies, waits for them, and re-layouts  22.3 us (15%)
  matrix products  20.3 us (14%)
  between operations  13.6 us (9%)
  starting transfers between devices  8.46 us (6%)
  other arithmetic  4.56 us (3%)
    reduce_scatter x1, waiting for transfers between devices, shards(): lax.psum_scatter(result + jnp.dot(selector, weighted, precision=lax.Preci...  69.6 us
    unnamed x12, local copies, waits for them, and re-layouts  15.8 us
    dot_general x2, matrix products, swiglu(): projected = jnp.dot(row_block, weights, preferred_element_type=jnp.float32)  9.49 us
    all_to_all x1, waiting for transfers between devices, shards(): lax.all_to_all(results.reshape(received.shape), 'expert', split_axis=0, c...  8.54 us
    dot_general x1, matrix products, shards(): jnp.dot(selector, weighted, precision=lax.Precision.HIGHEST)  5.54 us
    dot_general x1, matrix products, shards(): result = jnp.dot(hidden, shared_down, preferred_element_type=jnp.float32)  4.51 us
    all_to_all x1, starting transfers between devices, shards(): lax.all_to_all(results.reshape(received.shape), 'expert', split_axis=0, c...  4.22 us
    all_to_all x1, starting transfers between devices, shards(): lax.all_to_all(outgoing, 'expert', split_axis=0, concat_axis=0, tiled=True)  4.21 us
  transfers between devices with their start and end apart: 3, of which 2 were waited for; matrix products, arithmetic and copies ran while one was open for 17% of the time, Pallas kernels for 0%

commit v1 on v0

v1 whole, which is shorter than its diff:
```python
import functools

import jax
import jax.numpy as jnp
from jax import lax
from jax.experimental import pallas as pl
from jax.experimental.pallas import tpu as pltpu
from jax.sharding import PartitionSpec as P

BF16 = jnp.bfloat16
F32 = jnp.float32
I32 = jnp.int32
PIECE = 256
MIB = 1 << 20


def iota(shape, dim):
    return lax.broadcasted_iota(I32, shape, dim)


def dot(a, b):
    return jnp.dot(a, b, preferred_element_type=F32)


def in_hbm(*arrays):
    return [pltpu.with_memory_space_constraint(array, pltpu.HBM) for array in arrays]


def chunk_count(width):
    for count in (4, 2, 1):
        if width % (count * PIECE) == 0:
            return count
    raise ValueError(width)


def plan_kernel(experts, capacity, share_hbm, source_hbm, ids_hbm, gates_hbm, tokens_hbm, gate_out, tokens_ref, *rest):
    outs, (share_ref, source_ref, ids_ref, gates_ref, sems) = rest[:experts], rest[experts:]
    copies = [
        pltpu.make_async_copy(source, target, sems.at[number])
        for number, (source, target) in enumerate(
            [
                (ids_hbm, ids_ref),
                (share_hbm, share_ref),
                (source_hbm, source_ref),
                (gates_hbm, gates_ref),
                (tokens_hbm, tokens_ref),
            ]
        )
    ]
    for copy in copies:
        copy.start()
    for copy in copies[:-1]:
        copy.wait()
    ids = ids_ref[...]
    gates = gates_ref[...]
    top, rows = ids.shape
    me = lax.axis_index("expert")
    inside = ids < experts
    limit = jnp.zeros_like(ids)
    home = jnp.zeros_like(ids)
    for index in range(experts):
        limit = jnp.where(ids == index, share_ref[index], limit)
        home = jnp.where(ids == source_ref[index], index, home)
    by_copy = inside & (iota((top, rows), 1) < limit)
    holder = jnp.where(by_copy, home, ids)
    members = [jnp.where(inside & (holder == index), 1.0, 0.0) for index in range(experts)]
    earlier = jnp.where(iota((rows, rows), 0) < iota((rows, rows), 1), 1.0, 0.0).astype(BF16)
    rank = jnp.zeros((top, rows), F32)
    for index in range(experts):
        member = members[index]
        counts = jnp.broadcast_to(jnp.sum(member, axis=0, keepdims=True), (8, rows))
        running = dot(counts.astype(BF16), earlier)[:1]
        lines = []
        for k in range(top):
            lines.append(running)
            running = running + member[k : k + 1]
        rank = rank + member * jnp.concatenate(lines, axis=0)
    rank = rank.astype(I32)
    served = inside & (rank < capacity)
    slots = 2 * capacity
    place = jnp.where(served, ids * slots + rank + jnp.where(by_copy, capacity, 0), -1)
    seat = jnp.where(served, holder * capacity + rank, -1)
    seats = jnp.zeros((rows, rows), F32)
    for k in range(top):
        seats = seats + jnp.where(seat[k : k + 1] == iota((rows, rows), 0), gates[k : k + 1], 0.0)
    gate_out[...] = seats.T
    height = experts * 2 * slots
    line = iota((height, 1), 0)
    within = lax.rem(line, 2 * slots)
    wanted = (me ^ (line // (2 * slots))) * slots + lax.rem(within, slots)
    pick = jnp.zeros((height, rows), F32)
    for k in range(top):
        pick = pick + jnp.where(place[k : k + 1] == wanted, 1.0, 0.0)
    first = jnp.where(within < slots, pick, 0.0).astype(BF16)
    second = jnp.where(within < slots, 0.0, pick).astype(BF16)
    copies[-1].wait()
    half = tokens_ref.shape[1] // 2
    step = half // chunk_count(half) if half % PIECE == 0 else half
    for start in range(0, half, step):
        picked = dot(first, tokens_ref[:, start : start + step]) + dot(
            second, tokens_ref[:, half + start : half + start + step]
        )
        for index in range(experts):
            outs[index][:, start : start + step] = picked[
                index * 2 * slots : (index + 1) * 2 * slots
            ].astype(BF16)


def plan(route_ids, route_gates, copy_source, copy_share, tokens, experts, capacity):
    rows, width = tokens.shape
    vmem = pl.BlockSpec(memory_space=pltpu.VMEM)
    hbm = pl.BlockSpec(memory_space=pltpu.HBM)
    return pl.pallas_call(
        functools.partial(plan_kernel, experts, capacity),
        out_shape=[pltpu.VMEM((rows, rows), F32), pltpu.VMEM((rows, width), BF16)]
        + [pltpu.VMEM((4 * capacity, width // 2), BF16)] * experts,
        in_specs=[hbm] * 5,
        out_specs=[vmem] * (experts + 2),
        scratch_shapes=[
            pltpu.SMEM(copy_share.shape, I32),
            pltpu.SMEM(copy_source.shape, I32),
            pltpu.VMEM(route_ids.shape[::-1], I32),
            pltpu.VMEM(route_gates.shape[::-1], F32),
            pltpu.SemaphoreType.DMA((5,)),
        ],
        compiler_params=pltpu.CompilerParams(vmem_limit_bytes=16 * MIB),
        cost_estimate=pl.CostEstimate(flops=10**8, bytes_accessed=4 * 10**6, transcendentals=0),
        name="plan",
    )(*in_hbm(copy_share, copy_source, route_ids.T, route_gates.T, tokens))


def doubler():
    shape = (PIECE, 2 * PIECE)
    return jnp.where(iota(shape, 1) // 2 == iota(shape, 0), 1.0, 0.0).astype(BF16)


def spread(block, twice):
    parts = []
    for start in range(0, block.shape[1], PIECE):
        both = dot(block[:, start : start + PIECE], twice)
        even = lax.rem(iota(both.shape, 1), 2) == 0
        gate = jnp.where(even, both, 0.0).astype(BF16)
        up = jnp.where(even, 0.0, both).astype(BF16)
        parts.append(jnp.concatenate([gate, up], axis=0))
    return jnp.concatenate(parts, axis=1)


def gated(total):
    rows = total.shape[0] // 2
    gate = total[:rows]
    return gate / (1.0 + jnp.exp(-gate)) * total[rows:]


def line_plan(count):
    even, odd, table = {}, {}, []
    for phase in range(1, count):
        for parity, names in ((0, even), (1, odd)):
            need = {}
            for i in range(count):
                rises = i % 2 == parity
                other = i + 1 if rises else i - 1
                shard = count - phase + i if rises else i - count + phase
                if 0 <= other < count and (i <= phase - 1 if rises else i >= count - phase):
                    need[i] = shard
            if not need:
                continue
            for number, held in enumerate(table):
                if all(held.get(i, shard) == shard for i, shard in need.items()):
                    break
            else:
                number = len(table)
                table.append({})
            table[number].update(need)
            names[phase] = number
    table.append({i: i for i in range(count)})
    return even, odd, [[held.get(i, i) for i in range(count)] for held in table]


def shared_kernel(table, x_ref, up_hbm, down_hbm, late_hbm, *rest):
    outs, rest = rest[: len(table)], rest[len(table) :]
    late_ref, up_ref, down_ref, hidden_ref, up_sem, down_sem, late_sem = rest
    rows, width = x_ref.shape
    share = outs[0].shape[0]
    hidden_width = up_ref.shape[2]
    count = chunk_count(width)
    size = width // count
    up_copies, down_copies = [], []
    for c in range(count):
        part = pl.ds(c * size, size)
        up_copies.append(pltpu.make_async_copy(up_hbm.at[part], up_ref.at[part], up_sem.at[c]))
        up_copies[-1].start()
    for c in range(count):
        part = pl.ds(c * size, size)
        down_copies.append(
            pltpu.make_async_copy(down_hbm.at[:, part], down_ref.at[:, part], down_sem.at[c])
        )
        down_copies[-1].start()
    late = pltpu.make_async_copy(late_hbm, late_ref, late_sem)
    late.start()
    twice = doubler()
    total = None
    for c in range(count):
        left = spread(x_ref[:, c * size : (c + 1) * size], twice)
        up_copies[c].wait()
        product = dot(left, up_ref.at[pl.ds(c * size, size)].reshape(2 * size, hidden_width)[...])
        total = product if total is None else total + product
    hidden_ref[...] = gated(total).astype(BF16)
    index = lax.axis_index("replica")
    picked = []
    for held in table:
        number = jnp.int32(0)
        for i, shard in enumerate(held):
            number = jnp.where(index == i, shard, number)
        picked.append(hidden_ref[pl.ds(pl.multiple_of(number * share, share), share), :])
    hidden = jnp.concatenate(picked, axis=0)
    for c in range(count):
        down_copies[c].wait()
        result = dot(hidden, down_ref[:, c * size : (c + 1) * size]).astype(BF16)
        for number, out in enumerate(outs):
            out[:, c * size : (c + 1) * size] = result[number * share : (number + 1) * share]
    late.wait()


def shared(tokens, up, down, late, table):
    rows, width = tokens.shape
    count = chunk_count(width)
    share = rows // len(table[0])
    vmem = pl.BlockSpec(memory_space=pltpu.VMEM)
    return pl.pallas_call(
        functools.partial(shared_kernel, table),
        out_shape=[pltpu.VMEM((share, width), BF16)] * len(table)
        + [pltpu.VMEM(late.shape, BF16)],
        in_specs=[vmem] + [pl.BlockSpec(memory_space=pltpu.HBM)] * 3,
        out_specs=[vmem] * (len(table) + 1),
        scratch_shapes=[
            pltpu.VMEM(up.shape, BF16),
            pltpu.VMEM(down.shape, BF16),
            pltpu.VMEM((rows, down.shape[0]), BF16),
            pltpu.SemaphoreType.DMA((count,)),
            pltpu.SemaphoreType.DMA((count,)),
            pltpu.SemaphoreType.DMA,
        ],
        compiler_params=pltpu.CompilerParams(vmem_limit_bytes=24 * MIB),
        cost_estimate=pl.CostEstimate(flops=3 * 10**9, bytes_accessed=25 * 10**6, transcendentals=0),
        name="shared",
    )(tokens, *in_hbm(up, down, late))


def expert_kernel(count, *refs):
    parts, up_ref, down_hbm, outs = refs[:count], refs[count], refs[count + 1], refs[count + 2 : -2]
    down_ref, down_sem = refs[-2:]
    copy = pltpu.make_async_copy(down_hbm, down_ref, down_sem)
    copy.start()
    lines, half = parts[0].shape
    hidden_width = up_ref.shape[2]
    pieces = chunk_count(half) if half % PIECE == 0 else 1
    size = half // pieces
    twice = doubler()
    totals = []
    for side in range(2):
        total = None
        for c in range(pieces):
            block = jnp.concatenate([part[:, c * size : (c + 1) * size] for part in parts], axis=0)
            left = spread(block, twice)
            start = side * half + c * size
            product = dot(left, up_ref.at[pl.ds(start, size)].reshape(2 * size, hidden_width)[...])
            total = product if total is None else total + product
        totals.append(total)
    height = count * lines
    slots = lines // 2

    def shifted(a, by):
        return pltpu.roll(a, by % a.shape[0], 0)

    top = lax.rem(iota((height, 1), 0), lines) < slots
    total = totals[0] + shifted(totals[1], -slots)
    hidden = gated(total)
    hidden = jnp.where(top, hidden, shifted(hidden, slots)).astype(BF16)
    copy.wait()
    for c in range(pieces):
        start = c * size
        first = dot(hidden, down_ref[:, start : start + size])
        second = dot(hidden, down_ref[:, half + start : half + start + size])
        both = jnp.where(top, first, second)
        for index in range(count):
            outs[index][:, start : start + size] = both[index * lines : (index + 1) * lines].astype(
                BF16
            )


def run_expert(parts, up, down):
    count = len(parts)
    vmem = pl.BlockSpec(memory_space=pltpu.VMEM)
    return pl.pallas_call(
        functools.partial(expert_kernel, count),
        out_shape=[jax.ShapeDtypeStruct(parts[0].shape, BF16)] * count,
        in_specs=[vmem] * (count + 1) + [pl.BlockSpec(memory_space=pltpu.HBM)],
        out_specs=[vmem] * count,
        scratch_shapes=[pltpu.VMEM(down.shape, BF16), pltpu.SemaphoreType.DMA],
        compiler_params=pltpu.CompilerParams(vmem_limit_bytes=32 * MIB),
        cost_estimate=pl.CostEstimate(flops=6 * 10**10, bytes_accessed=13 * 10**6, transcendentals=0),
        name="routed",
    )(*parts, up, *in_hbm(down))


def seat_kernel(count, capacity, source_ref, *refs):
    parts, keep_ref, send_ref = refs[:count], refs[count], refs[count + 1]
    lines, half = parts[0].shape
    slots = lines // 2
    me = lax.axis_index("expert")
    side = lax.rem(lax.axis_index("replica"), 2)
    shape = (count * capacity, count * lines)
    seat, line = iota(shape, 0), iota(shape, 1)
    within = lax.rem(line, lines)
    slot = lax.rem(within, slots)
    expert = me ^ (line // lines)
    home = jnp.zeros(shape, I32)
    for index in range(count):
        home = jnp.where(expert == source_ref[index], index, home)
    target = jnp.where(slot < capacity, expert * capacity + slot, home * capacity + slot - capacity)
    here = (target == seat).astype(F32)
    second = (within >= slots).astype(I32)
    keep = jnp.where(second == side, here, 0.0).astype(BF16)
    send = jnp.where(second == side, 0.0, here).astype(BF16)
    pieces = chunk_count(half) if half % PIECE == 0 else 1
    size = half // pieces
    for c in range(pieces):
        cols = slice(c * size, (c + 1) * size)
        block = jnp.concatenate([part[:, cols] for part in parts], axis=0)
        keep_ref[:, cols] = dot(keep, block).astype(BF16)
        send_ref[:, cols] = dot(send, block).astype(BF16)


def seat_answers(parts, copy_source, capacity):
    count = len(parts)
    vmem = pl.BlockSpec(memory_space=pltpu.VMEM)
    shape = jax.ShapeDtypeStruct((count * capacity, parts[0].shape[1]), BF16)
    return pl.pallas_call(
        functools.partial(seat_kernel, count, capacity),
        out_shape=[shape, shape],
        in_specs=[pl.BlockSpec(memory_space=pltpu.SMEM)] + [vmem] * count,
        out_specs=[vmem, vmem],
        compiler_params=pltpu.CompilerParams(vmem_limit_bytes=16 * MIB),
        cost_estimate=pl.CostEstimate(flops=10**8, bytes_accessed=2 * 10**6, transcendentals=0),
        name="seats",
    )(copy_source, *parts)


def mix_kernel(own_ref, even_ref, odd_ref, gate_ref, mine_ref, other_ref, out_ref):
    side = lax.rem(lax.axis_index("replica"), 2)
    seats, half = mine_ref.shape
    gates = gate_ref[:, :seats]
    high = gates.astype(BF16)
    left = gates - high.astype(F32)
    middle = left.astype(BF16)
    low = (left - middle.astype(F32)).astype(BF16)
    for position in range(2):
        cols = slice(position * half, (position + 1) * half)
        answers = jnp.where(side == position, mine_ref[...], other_ref[...])
        routed = dot(high, answers) + dot(middle, answers) + dot(low, answers)
        base = own_ref[:, cols].astype(F32) + even_ref[:, cols].astype(F32) + odd_ref[:, cols].astype(F32)
        out_ref[:, cols] = (base + routed).astype(BF16)


def mix(own, even, odd, gates, mine, other):
    vmem = pl.BlockSpec(memory_space=pltpu.VMEM)
    return pl.pallas_call(
        mix_kernel,
        out_shape=jax.ShapeDtypeStruct(own.shape, BF16),
        in_specs=[vmem] * 6,
        out_specs=vmem,
        compiler_params=pltpu.CompilerParams(vmem_limit_bytes=16 * MIB),
        cost_estimate=pl.CostEstimate(flops=10**8, bytes_accessed=2 * 10**6, transcendentals=0),
        name="mix",
    )(own, even, odd, gates, mine, other)


def swap(array, axis, distance):
    pairs = [(i, i ^ distance) for i in range(lax.axis_size(axis))]
    return lax.ppermute(array, axis, pairs)


def add(a, b):
    return (a.astype(F32) + b.astype(F32)).astype(BF16)


def shards(
    tokens,
    route_ids,
    route_gates,
    copy_source,
    copy_share,
    w_gate_up,
    w_down,
    shared_gate_up,
    shared_down,
):
    experts = lax.axis_size("expert")
    replicas = lax.axis_size("replica")
    rows = tokens.shape[0]
    capacity = max(2, rows * 3 // 64)
    even, odd, table = line_plan(replicas)
    even_pairs = [(i, i ^ 1) for i in range(replicas)]
    odd_pairs = [(i, i + 1 if i % 2 else i - 1) for i in range(1, replicas - 1)]
    gates, tokens, *outgoing = plan(
        route_ids, route_gates, copy_source, copy_share, tokens, experts, capacity
    )
    incoming = [outgoing[0]] + [swap(outgoing[d], "expert", d) for d in range(1, experts)]
    *parts, up = shared(tokens, shared_gate_up, shared_down, w_gate_up[0], table)
    got_even = got_odd = None

    def phase(number, got_even, got_odd):
        send_even, send_odd = parts[even[number]], None
        if got_odd is not None:
            send_even = add(send_even, got_odd)
        elif got_even is not None:
            send_even, got_even = lax.optimization_barrier((send_even, got_even))
        if number in odd:
            send_odd = add(parts[odd[number]], got_even)
        got_even = lax.ppermute(send_even, "replica", even_pairs)
        got_odd = lax.ppermute(send_odd, "replica", odd_pairs) if number in odd else None
        return got_even, got_odd

    got_even, got_odd = phase(1, None, None)
    results = run_expert(incoming, up, w_down[0])
    answers = [results[0]] + [swap(results[d], "expert", d) for d in range(1, experts)]
    if replicas > 2:
        near = min(2, experts - 1)
        got_even, answers[near] = lax.optimization_barrier((got_even, answers[near]))
        got_even, got_odd = phase(2, got_even, got_odd)
    keep, send = seat_answers(answers, copy_source, capacity)
    got = swap(send, "replica", 1)
    for number in range(3, replicas):
        got_even, got_odd, keep = lax.optimization_barrier((got_even, got_odd, keep))
        got_even, got_odd = phase(number, got_even, got_odd)
    mine = add(keep, got)
    distance = 2
    while distance < replicas:
        mine = add(mine, swap(mine, "replica", distance))
        distance *= 2
    other = swap(mine, "replica", 1)
    share = rows // replicas
    own_gates = lax.dynamic_slice_in_dim(gates, lax.axis_index("replica") * share, share, 0)
    if got_odd is None:
        got_odd = jnp.zeros_like(got_even)
    return mix(parts[-1], got_even, got_odd, own_gates, mine, other)


def solution(mesh):
    return jax.shard_map(
        shards,
        mesh=mesh,
        in_specs=(
            P(("group", "expert"), None),
            P(("group", "expert"), None),
            P(("group", "expert"), None),
            P("group"),
            P("group"),
            P("expert", None, None, "replica"),
            P("expert", "replica", None),
            P(None, None, "replica"),
            P("replica", None),
        ),
        out_specs=P(("group", "expert", "replica"), None),
        check_vma=False,
    )
```

time: 148 us -> 71.1 us (0.48)
  waiting for transfers between devices: 78.2 us -> 33.1 us
  local copies, waits for them, and re-layouts: 22.3 us -> 0.02 us
  matrix products: 20.3 us -> 0 us
  Pallas kernels: 0 us -> 18 us
  between operations: 13.6 us -> 0.12 us
  starting transfers between devices: 8.46 us -> 19.2 us
  other arithmetic: 4.56 us -> 0.41 us
    reduce_scatter x1 -> x0, waiting for transfers between devices: 69.6 us -> none  [shards(): lax.psum_scatter(result + jnp.dot(selector, weighted, precision=lax.Preci...]
    ppermute x0 -> x14, waiting for transfers between devices: none -> 33.1 us  [the longest x9 30.7 us: swap(): return lax.ppermute(array, axis, pairs)]
    dot_general x5 -> x0, matrix products: 20.3 us -> none  [the longest x2 9.49 us: swiglu(): projected = jnp.dot(row_block, weights, preferred_element_type=jnp.float32)]
    ppermute x0 -> x14, starting transfers between devices: none -> 19.2 us  [the longest x3 10.3 us: phase(): got_even = lax.ppermute(send_even, 'replica', even_pairs)]
    pallas_call x0 -> x5, Pallas kernels: none -> 18 us  [the longest x1 7.78 us: shared(): pl.pallas_call(functools.partial(shared_kernel, table), out_shape=[pltpu....]
    unnamed x12 -> x2, local copies, waits for them, and re-layouts: 15.8 us -> 0.01 us
    all_to_all x2 -> x0, waiting for transfers between devices: 8.54 us -> none  [the longest x1 8.54 us: shards(): lax.all_to_all(results.reshape(received.shape), 'expert', split_axis=0, c...]
    all_to_all x2 -> x0, starting transfers between devices: 8.42 us -> none  [the longest x1 4.22 us: shards(): lax.all_to_all(results.reshape(received.shape), 'expert', split_axis=0, c...]
  transfers between devices with their start and end apart: 3 -> 14, of which waited for: 2 -> 6; matrix products, arithmetic and copies ran while one was open for 17% -> 0% of each run, Pallas kernels for 0% -> 21%
where the time goes in v1:
time: 71.1 us; the launch traced here: 70.9 us
  waiting for transfers between devices  33.1 us (47%)
  starting transfers between devices  19.2 us (27%)
  Pallas kernels  18 us (25%)
    ppermute x9, waiting for transfers between devices, swap(): return lax.ppermute(array, axis, pairs)  30.7 us
    ppermute x3, starting transfers between devices, phase(): got_even = lax.ppermute(send_even, 'replica', even_pairs)  10.3 us
    pallas_call x1, Pallas kernels, shared(): pl.pallas_call(functools.partial(shared_kernel, table), out_shape=[pltpu....  7.78 us
    ppermute x9, starting transfers between devices, swap(): return lax.ppermute(array, axis, pairs)  7.49 us
    pallas_call x1, Pallas kernels, run_expert(): pl.pallas_call(functools.partial(expert_kernel, count), out_shape=[jax.Sh...  5.95 us
    ppermute x3, waiting for transfers between devices, phase(): got_even = lax.ppermute(send_even, 'replica', even_pairs)  2.41 us
    pallas_call x1, Pallas kernels, plan(): pl.pallas_call(functools.partial(plan_kernel, experts, capacity), out_sha...  2.09 us
  transfers between devices with their start and end apart: 14, of which 6 were waited for; matrix products, arithmetic and copies ran while one was open for 0% of the time, Pallas kernels for 21%

profile of v1, /device:TPU:0, one launch (start us, length us, event | category | flops | bytes accessed | tf_op | source)
XLA Modules:
  0.0 70.9 jit_solution(17566265183399140330)
XLA Ops:
  0.0 2.1 %plan.1 = (f32[128,128]{1,0:T(8,128)S(1)}, bf16[128,7168]{1,0:T(8,128)(2,1)S(1)}, bf16[24,3584]{1,0:T(8,128)(2,1)S(1)}, bf16[24,3584]{1,0:T(8,128)(2,1)S(1)}, bf...) custom-call(s32[4]{0:T(128)} %share_hbm.1, s32[4]{0:T(128)} %source_ref.1, s32[8,128]{1,0:T(8,128)} %bitcast.5, ...), custom_call_target="tpu_custom_call" | custom-call | flops 100000000 | bytes 4000000 | tf_op jit(solution)/shard_map/plan/pallas_call | solution.py:113
  2.1 0.5 collective-permute-start.1
  2.6 2.6 %collective-permute-start.2 = (bf16[24,3584]{1,0:T(8,128)(2,1)S(1)}, bf16[24,3584]{1,0:T(8,128)(2,1)S(1)}, u32[]{:S(2)}, u32[]{:S(2)}) collective-permute-start(bf16[24,3584]{1,0:T(8,128)(2,1)S(1)} %get-tuple-element.36), channel_id=1, source_target_pairs={{0,8},{4,12},{8,0},{12,4},{1,9},{5,13},{9,1},{13,5},{2,10},{6,14},... | collective-permute-start | bytes 516104 | tf_op jit(solution)/shard_map/ppermute | solution.py:380
  5.2 0.1 collective-permute-start.3
  5.3 7.8 %shared.1 = (bf16[32,7168]{1,0:T(8,128)(2,1)S(1)}, bf16[32,7168]{1,0:T(8,128)(2,1)S(1)}, bf16[32,7168]{1,0:T(8,128)(2,1)S(1)}, bf16[32,7168]{1,0:T(8,128)(2,1)S(1)}, bf16[7168,2,256]{2,1,0:T(2,128)(2,1)S(1)}) custom-call(bf16[128,7168]{1,0:T(8,128)(2,1)S(1)} %get-tuple-element.29.x_ref, bf16[7168,2,256]{2,1,0:T(2,128)(2,1)} %up_hbm.1, ...), custom_call_target="tpu_custom_call" | custom-call | flops 3000000000 | bytes 25000000 | tf_op jit(solution)/shard_map/shared/pallas_call | solution.py:229
  13.0 1.9 %collective-permute-start = (bf16[32,7168]{1,0:T(8,128)(2,1)S(1)}, bf16[32,7168]{1,0:T(8,128)(2,1)S(1)}, u32[]{:S(2)}, u32[]{:S(2)}) collective-permute-start(bf16[32,7168]{1,0:T(8,128)(2,1)S(1)} %get-tuple-element.33), channel_id=1, source_target_pairs={{0,1},{1,0},{2,3},{3,2},{4,5},{5,4},{6,7},{7,6},{8,9},{9,8},{10,11... | collective-permute-start | bytes 1376264 | tf_op jit(solution)/shard_map/ppermute | solution.py:420
  14.9 0.0 collective-permute-done.1.refs_1_
  14.9 0.0 collective-permute-done.2.refs_2_
  14.9 0.0 collective-permute-done.3.refs_3_
  14.9 0.0 copy-start
  15.0 6.0 %routed.1 = (bf16[24,3584]{1,0:T(8,128)(2,1)S(1)}, bf16[24,3584]{1,0:T(8,128)(2,1)S(1)}, bf16[24,3584]{1,0:T(8,128)(2,1)S(1)}, bf16[24,3584]{1,0:T(8,128)(2,1)S(1)}) custom-call(bf16[24,3584]{1,0:T(8,128)(2,1)S(1)} %get-tuple-element.34.refs_0_, bf16[24,3584]{1,0:T(8,128)(2,1)S(1)} %collective-permute-done.1.refs_1_, ...), custom_call_target="tpu_custom_call" | custom-call | flops 60000002048 | bytes 13000000 | tf_op jit(solution)/shard_map/routed/pallas_call | solution.py:294
  20.9 1.6 %collective-permute-start.4 = (bf16[24,3584]{1,0:T(8,128)(2,1)S(1)}, bf16[24,3584]{1,0:T(8,128)(2,1)S(1)}, u32[]{:S(2)}, u32[]{:S(2)}) collective-permute-start(bf16[24,3584]{1,0:T(8,128)(2,1)S(1)} %get-tuple-element.39), channel_id=1, source_target_pairs={{0,8},{4,12},{8,0},{12,4},{1,9},{5,13},{9,1},{13,5},{2,10},{6,14},... | collective-permute-start | bytes 516104 | tf_op jit(solution)/shard_map/ppermute | solution.py:380
  22.5 4.8 %collective-permute-done.4.refs_2_ = bf16[24,3584]{1,0:T(8,128)(2,1)S(1)} collective-permute-done((bf16[24,3584]{1,0:T(8,128)(2,1)S(1)}, bf16[24,3584]{1,0:T(8,128)(2,1)S(1)}, u32[]{:S(2)}, u32[]{:S(2)}) %collective-permute-start.4) | collective-permute-done | bytes 172064 | tf_op jit(solution)/shard_map/ppermute | solution.py:380
  27.3 0.0 collective-permute-done
  27.3 0.1 add_convert_fusion.2
  27.4 0.7 collective-permute-start.6
  28.1 4.4 %collective-permute-start.5 = (bf16[32,7168]{1,0:T(8,128)(2,1)S(1)}, bf16[32,7168]{1,0:T(8,128)(2,1)S(1)}, u32[]{:S(2)}, u32[]{:S(2)}) collective-permute-start(bf16[32,7168]{1,0:T(8,128)(2,1)S(1)} %get-tuple-element.41), channel_id=1, source_target_pairs={{0,1},{1,0},{2,3},{3,2},{4,5},{5,4},{6,7},{7,6},{8,9},{9,8},{10,11... | collective-permute-start | bytes 1376264 | tf_op jit(solution)/shard_map/ppermute | solution.py:420
  32.6 0.0 collective-permute-start.7
  32.6 1.6 %collective-permute-start.8 = (bf16[24,3584]{1,0:T(8,128)(2,1)S(1)}, bf16[24,3584]{1,0:T(8,128)(2,1)S(1)}, u32[]{:S(2)}, u32[]{:S(2)}) collective-permute-start(bf16[24,3584]{1,0:T(8,128)(2,1)S(1)} %get-tuple-element.46), channel_id=1, source_target_pairs={{0,12},{4,8},{8,4},{12,0},{1,13},{5,9},{9,5},{13,1},{2,14},{6,10},... | collective-permute-start | bytes 516104 | tf_op jit(solution)/shard_map/ppermute | solution.py:380
  34.2 0.0 collective-permute-done.7.refs_1_
  34.2 4.4 %collective-permute-done.8.refs_3_ = bf16[24,3584]{1,0:T(8,128)(2,1)S(1)} collective-permute-done((bf16[24,3584]{1,0:T(8,128)(2,1)S(1)}, bf16[24,3584]{1,0:T(8,128)(2,1)S(1)}, u32[]{:S(2)}, u32[]{:S(2)}) %collective-permute-start.8) | collective-permute-done | bytes 172064 | tf_op jit(solution)/shard_map/ppermute | solution.py:380
  38.6 0.0 copy-done
  38.6 0.9 %seats.1 = (bf16[24,3584]{1,0:T(8,128)(2,1)S(1)}, bf16[24,3584]{1,0:T(8,128)(2,1)S(1)}) custom-call(s32[4]{0:T(128)S(1)} %copy-done, bf16[24,3584]{1,0:T(8,128)(2,1)S(1)} %get-tuple-element.43.refs_0_, bf16[24,3584]{1,0:T(8,128)(2,1)S(1)} %collective-permute-done.7.refs_1_, bf16[24,3584]{1,0:T(8,128)(2,1)S(1)} %collective-permute-done.4.refs_2_, ...), custom_call_target="tpu_custom_call" | custom-call | flops 100000000 | bytes 2000000 | tf_op jit(solution)/shard_map/seats/pallas_call | solution.py:338
  39.5 0.3 collective-permute-start.11
  39.8 0.0 collective-permute-done.6
  39.8 2.4 %collective-permute-done.5 = bf16[32,7168]{1,0:T(8,128)(2,1)S(1)} collective-permute-done((bf16[32,7168]{1,0:T(8,128)(2,1)S(1)}, bf16[32,7168]{1,0:T(8,128)(2,1)S(1)}, u32[]{:S(2)}, u32[]{:S(2)}) %collective-permute-start.5) | collective-permute-done | bytes 458784 | tf_op jit(solution)/shard_map/ppermute | solution.py:420
  42.2 0.1 add_convert_fusion
  42.3 4.3 %collective-permute-done.11 = bf16[24,3584]{1,0:T(8,128)(2,1)S(1)} collective-permute-done((bf16[24,3584]{1,0:T(8,128)(2,1)S(1)}, bf16[24,3584]{1,0:T(8,128)(2,1)S(1)}, u32[]{:S(2)}, u32[]{:S(2)}) %collective-permute-start.11) | collective-permute-done | bytes 172064 | tf_op jit(solution)/shard_map/ppermute | solution.py:380
  46.6 0.8 %collective-permute-start.12 = (bf16[24,3584]{1,0:T(8,128)(2,1)S(1)}, bf16[24,3584]{1,0:T(8,128)(2,1)S(1)}, u32[]{:S(2)}, u32[]{:S(2)}) collective-permute-start(bf16[24,3584]{1,0:T(8,128)(2,1)S(1)} %add_convert_fusion.4), channel_id=1, source_target_pairs={{0,2},{1,3},{2,0},{3,1},{4,6},{5,7},{6,4},{7,5},{8,10},{9,11},{10,... | collective-permute-start | bytes 516104 | tf_op jit(solution)/shard_map/ppermute | solution.py:380
  47.4 0.7 collective-permute-start.10
  48.1 0.1 add_convert_fusion.1
  48.2 4.0 %collective-permute-start.9 = (bf16[32,7168]{1,0:T(8,128)(2,1)S(1)}, bf16[32,7168]{1,0:T(8,128)(2,1)S(1)}, u32[]{:S(2)}, u32[]{:S(2)}) collective-permute-start(bf16[32,7168]{1,0:T(8,128)(2,1)S(1)} %add_convert_fusion.1), channel_id=1, source_target_pairs={{0,1},{1,0},{2,3},{3,2},{4,5},{5,4},{6,7},{7,6},{8,9},{9,8},{10,11... | collective-permute-start | bytes 1376264 | tf_op jit(solution)/shard_map/ppermute | solution.py:420
  52.3 5.3 %collective-permute-done.12 = bf16[24,3584]{1,0:T(8,128)(2,1)S(1)} collective-permute-done((bf16[24,3584]{1,0:T(8,128)(2,1)S(1)}, bf16[24,3584]{1,0:T(8,128)(2,1)S(1)}, u32[]{:S(2)}, u32[]{:S(2)}) %collective-permute-start.12) | collective-permute-done | bytes 172064 | tf_op jit(solution)/shard_map/ppermute | solution.py:380
  57.6 0.1 collective-permute-start.13
  57.7 11.8 %collective-permute-done.13.other_ref = bf16[24,3584]{1,0:T(8,128)(2,1)S(1)} collective-permute-done((bf16[24,3584]{1,0:T(8,128)(2,1)S(1)}, bf16[24,3584]{1,0:T(8,128)(2,1)S(1)}, u32[]{:S(2)}, u32[]{:S(2)}) %collective-permute-start.13) | collective-permute-done | bytes 172064 | tf_op jit(solution)/shard_map/ppermute | solution.py:380
  69.6 0.0 collective-permute-done.10.odd_ref
  69.6 0.0 collective-permute-done.9.even_ref
  69.6 1.3 %mix.1 = bf16[32,7168]{1,0:T(8,128)(2,1)} custom-call(bf16[32,7168]{1,0:T(8,128)(2,1)S(1)} %get-tuple-element.30.own_ref, bf16[32,7168]{1,0:T(8,128)(2,1)S(1)} %collective-permute-done.9.even_ref, bf16[32,7168]{1,0:T(8,128)(2,1)S(1)} %collective-permute-done.10.odd_ref, f32[32,128]{1,0:T(8,128)S(1)} %constant_dynamic-slice_fusion.gate_ref, ...), custom_call_target="tpu_custom_call" | custom-call | flops 100000000 | bytes 2000000 | tf_op jit(solution)/shard_map/mix/pallas_call | solution.py:367
  (3 shorter events, 0.1 us)
Async XLA Ops:
  2.1 12.8 %collective-permute-start.1 = (bf16[24,3584]{1,0:T(8,128)(2,1)S(1)}, bf16[24,3584]{1,0:T(8,128)(2,1)S(1)}, u32[]{:S(2)}, u32[]{:S(2)}) collective-permute-start(bf16[24,3584]{1,0:T(8,128)(2,1)S(1)} %get-tuple-element.35), channel_id=1, source_target_pairs={{0,4},{4,0},{8,12},{12,8},{1,5},{5,1},{9,13},{13,9},{2,6},{6,2},{1... | collective-permute-start | bytes 516104 | tf_op jit(solution)/shard_map/ppermute | solution.py:380
  2.6 12.3 %collective-permute-start.2 = (bf16[24,3584]{1,0:T(8,128)(2,1)S(1)}, bf16[24,3584]{1,0:T(8,128)(2,1)S(1)}, u32[]{:S(2)}, u32[]{:S(2)}) collective-permute-start(bf16[24,3584]{1,0:T(8,128)(2,1)S(1)} %get-tuple-element.36), channel_id=1, source_target_pairs={{0,8},{4,12},{8,0},{12,4},{1,9},{5,13},{9,1},{13,5},{2,10},{6,14},... | collective-permute-start | bytes 516104 | tf_op jit(solution)/shard_map/ppermute | solution.py:380
  5.2 9.8 %collective-permute-start.3 = (bf16[24,3584]{1,0:T(8,128)(2,1)S(1)}, bf16[24,3584]{1,0:T(8,128)(2,1)S(1)}, u32[]{:S(2)}, u32[]{:S(2)}) collective-permute-start(bf16[24,3584]{1,0:T(8,128)(2,1)S(1)} %get-tuple-element.37), channel_id=1, source_target_pairs={{0,12},{4,8},{8,4},{12,0},{1,13},{5,9},{9,5},{13,1},{2,14},{6,10},... | collective-permute-start | bytes 516104 | tf_op jit(solution)/shard_map/ppermute | solution.py:380
  13.0 14.3 %collective-permute-start = (bf16[32,7168]{1,0:T(8,128)(2,1)S(1)}, bf16[32,7168]{1,0:T(8,128)(2,1)S(1)}, u32[]{:S(2)}, u32[]{:S(2)}) collective-permute-start(bf16[32,7168]{1,0:T(8,128)(2,1)S(1)} %get-tuple-element.33), channel_id=1, source_target_pairs={{0,1},{1,0},{2,3},{3,2},{4,5},{5,4},{6,7},{7,6},{8,9},{9,8},{10,11... | collective-permute-start | bytes 1376264 | tf_op jit(solution)/shard_map/ppermute | solution.py:420
  14.9 23.7 %copy-start = (s32[4]{0:T(128)S(1)}, s32[4]{0:T(128)}, u32[]{:S(2)}) copy-start(s32[4]{0:T(128)} %source_ref.1) | copy-start | bytes 52
  20.9 6.4 %collective-permute-start.4 = (bf16[24,3584]{1,0:T(8,128)(2,1)S(1)}, bf16[24,3584]{1,0:T(8,128)(2,1)S(1)}, u32[]{:S(2)}, u32[]{:S(2)}) collective-permute-start(bf16[24,3584]{1,0:T(8,128)(2,1)S(1)} %get-tuple-element.39), channel_id=1, source_target_pairs={{0,8},{4,12},{8,0},{12,4},{1,9},{5,13},{9,1},{13,5},{2,10},{6,14},... | collective-permute-start | bytes 516104 | tf_op jit(solution)/shard_map/ppermute | solution.py:380
  27.4 12.3 %collective-permute-start.6 = (bf16[32,7168]{1,0:T(8,128)(2,1)S(1)}, bf16[32,7168]{1,0:T(8,128)(2,1)S(1)}, u32[]{:S(2)}, u32[]{:S(2)}) collective-permute-start(bf16[32,7168]{1,0:T(8,128)(2,1)S(1)} %add_convert_fusion.2), channel_id=1, source_target_pairs={{1,2},{2,1},{5,6},{6,5},{9,10},{10,9},{13,14},{14,13},{17,18},{18,... | collective-permute-start | bytes 1376264 | tf_op jit(solution)/shard_map/ppermute | solution.py:421
  28.1 14.0 %collective-permute-start.5 = (bf16[32,7168]{1,0:T(8,128)(2,1)S(1)}, bf16[32,7168]{1,0:T(8,128)(2,1)S(1)}, u32[]{:S(2)}, u32[]{:S(2)}) collective-permute-start(bf16[32,7168]{1,0:T(8,128)(2,1)S(1)} %get-tuple-element.41), channel_id=1, source_target_pairs={{0,1},{1,0},{2,3},{3,2},{4,5},{5,4},{6,7},{7,6},{8,9},{9,8},{10,11... | collective-permute-start | bytes 1376264 | tf_op jit(solution)/shard_map/ppermute | solution.py:420
  32.6 1.6 %collective-permute-start.7 = (bf16[24,3584]{1,0:T(8,128)(2,1)S(1)}, bf16[24,3584]{1,0:T(8,128)(2,1)S(1)}, u32[]{:S(2)}, u32[]{:S(2)}) collective-permute-start(bf16[24,3584]{1,0:T(8,128)(2,1)S(1)} %get-tuple-element.44), channel_id=1, source_target_pairs={{0,4},{4,0},{8,12},{12,8},{1,5},{5,1},{9,13},{13,9},{2,6},{6,2},{1... | collective-permute-start | bytes 516104 | tf_op jit(solution)/shard_map/ppermute | solution.py:380
  32.6 6.0 %collective-permute-start.8 = (bf16[24,3584]{1,0:T(8,128)(2,1)S(1)}, bf16[24,3584]{1,0:T(8,128)(2,1)S(1)}, u32[]{:S(2)}, u32[]{:S(2)}) collective-permute-start(bf16[24,3584]{1,0:T(8,128)(2,1)S(1)} %get-tuple-element.46), channel_id=1, source_target_pairs={{0,12},{4,8},{8,4},{12,0},{1,13},{5,9},{9,5},{13,1},{2,14},{6,10},... | collective-permute-start | bytes 516104 | tf_op jit(solution)/shard_map/ppermute | solution.py:380
  39.5 7.1 %collective-permute-start.11 = (bf16[24,3584]{1,0:T(8,128)(2,1)S(1)}, bf16[24,3584]{1,0:T(8,128)(2,1)S(1)}, u32[]{:S(2)}, u32[]{:S(2)}) collective-permute-start(bf16[24,3584]{1,0:T(8,128)(2,1)S(1)} %get-tuple-element.52), channel_id=1, source_target_pairs={{0,1},{1,0},{2,3},{3,2},{4,5},{5,4},{6,7},{7,6},{8,9},{9,8},{10,11... | collective-permute-start | bytes 516104 | tf_op jit(solution)/shard_map/ppermute | solution.py:380
  46.6 11.0 %collective-permute-start.12 = (bf16[24,3584]{1,0:T(8,128)(2,1)S(1)}, bf16[24,3584]{1,0:T(8,128)(2,1)S(1)}, u32[]{:S(2)}, u32[]{:S(2)}) collective-permute-start(bf16[24,3584]{1,0:T(8,128)(2,1)S(1)} %add_convert_fusion.4), channel_id=1, source_target_pairs={{0,2},{1,3},{2,0},{3,1},{4,6},{5,7},{6,4},{7,5},{8,10},{9,11},{10,... | collective-permute-start | bytes 516104 | tf_op jit(solution)/shard_map/ppermute | solution.py:380
  47.4 22.1 %collective-permute-start.10 = (bf16[32,7168]{1,0:T(8,128)(2,1)S(1)}, bf16[32,7168]{1,0:T(8,128)(2,1)S(1)}, u32[]{:S(2)}, u32[]{:S(2)}) collective-permute-start(bf16[32,7168]{1,0:T(8,128)(2,1)S(1)} %add_convert_fusion), channel_id=1, source_target_pairs={{1,2},{2,1},{5,6},{6,5},{9,10},{10,9},{13,14},{14,13},{17,18},{18,... | collective-permute-start | bytes 1376264 | tf_op jit(solution)/shard_map/ppermute | solution.py:421
  48.2 21.3 %collective-permute-start.9 = (bf16[32,7168]{1,0:T(8,128)(2,1)S(1)}, bf16[32,7168]{1,0:T(8,128)(2,1)S(1)}, u32[]{:S(2)}, u32[]{:S(2)}) collective-permute-start(bf16[32,7168]{1,0:T(8,128)(2,1)S(1)} %add_convert_fusion.1), channel_id=1, source_target_pairs={{0,1},{1,0},{2,3},{3,2},{4,5},{5,4},{6,7},{7,6},{8,9},{9,8},{10,11... | collective-permute-start | bytes 1376264 | tf_op jit(solution)/shard_map/ppermute | solution.py:420
  57.6 11.9 %collective-permute-start.13 = (bf16[24,3584]{1,0:T(8,128)(2,1)S(1)}, bf16[24,3584]{1,0:T(8,128)(2,1)S(1)}, u32[]{:S(2)}, u32[]{:S(2)}) collective-permute-start(bf16[24,3584]{1,0:T(8,128)(2,1)S(1)} %add_convert_fusion.3.mine_ref), channel_id=1, source_target_pairs={{0,1},{1,0},{2,3},{3,2},{4,5},{5,4},{6,7},{7,6},{8,9},{9,8},{10,11... | collective-permute-start | bytes 516104 | tf_op jit(solution)/shard_map/ppermute | solution.py:380

commit v2 on v1

--- a/solution.py
+++ b/solution.py
@@ -33,8 +33,24 @@
     raise ValueError(width)
 
 
-def plan_kernel(experts, capacity, share_hbm, source_hbm, ids_hbm, gates_hbm, tokens_hbm, gate_out, tokens_ref, *rest):
-    outs, (share_ref, source_ref, ids_ref, gates_ref, sems) = rest[:experts], rest[experts:]
+def scatter_rows(outs, columns, values):
+    first = 0
+    for out in outs:
+        last = first + out.shape[0]
+        out[:, columns] = values[first:last].astype(BF16)
+        first = last
+
+
+def bundles(experts, lines, width):
+    half = max(1, experts // 2)
+    heights = [lines] * half + [lines * (experts - half)] * (experts > half)
+    return [pltpu.VMEM((height, width), BF16) for height in heights]
+
+
+def plan_kernel(
+    experts, capacity, share_hbm, source_hbm, ids_hbm, gates_hbm, tokens_hbm, up_hbm, gate_out, tokens_ref, head_ref, *rest
+):
+    *outs, share_ref, source_ref, ids_ref, gates_ref, sems = rest
     copies = [
         pltpu.make_async_copy(source, target, sems.at[number])
         for number, (source, target) in enumerate(
@@ -44,12 +60,13 @@
                 (source_hbm, source_ref),
                 (gates_hbm, gates_ref),
                 (tokens_hbm, tokens_ref),
+                (up_hbm.at[pl.ds(0, head_ref.shape[0])], head_ref),
             ]
         )
     ]
     for copy in copies:
         copy.start()
-    for copy in copies[:-1]:
+    for copy in copies[:4]:
         copy.wait()
     ids = ids_ref[...]
     gates = gates_ref[...]
@@ -93,40 +110,43 @@
         pick = pick + jnp.where(place[k : k + 1] == wanted, 1.0, 0.0)
     first = jnp.where(within < slots, pick, 0.0).astype(BF16)
     second = jnp.where(within < slots, 0.0, pick).astype(BF16)
-    copies[-1].wait()
+    copies[4].wait()
     half = tokens_ref.shape[1] // 2
     step = half // chunk_count(half) if half % PIECE == 0 else half
     for start in range(0, half, step):
         picked = dot(first, tokens_ref[:, start : start + step]) + dot(
             second, tokens_ref[:, half + start : half + start + step]
         )
-        for index in range(experts):
-            outs[index][:, start : start + step] = picked[
-                index * 2 * slots : (index + 1) * 2 * slots
-            ].astype(BF16)
-
-
-def plan(route_ids, route_gates, copy_source, copy_share, tokens, experts, capacity):
+        scatter_rows(outs, slice(start, start + step), picked)
+    copies[5].wait()
+
+
+def plan(route_ids, route_gates, copy_source, copy_share, tokens, up, experts, capacity):
     rows, width = tokens.shape
+    sent = bundles(experts, 4 * capacity, width // 2)
     vmem = pl.BlockSpec(memory_space=pltpu.VMEM)
     hbm = pl.BlockSpec(memory_space=pltpu.HBM)
     return pl.pallas_call(
         functools.partial(plan_kernel, experts, capacity),
-        out_shape=[pltpu.VMEM((rows, rows), F32), pltpu.VMEM((rows, width), BF16)]
-        + [pltpu.VMEM((4 * capacity, width // 2), BF16)] * experts,
-        in_specs=[hbm] * 5,
-        out_specs=[vmem] * (experts + 2),
+        out_shape=[
+            pltpu.VMEM((rows, rows), F32),
+            pltpu.VMEM((rows, width), BF16),
+            pltpu.VMEM((width // 2,) + up.shape[1:], BF16),
+        ]
+        + sent,
+        in_specs=[hbm] * 6,
+        out_specs=[vmem] * (len(sent) + 3),
         scratch_shapes=[
             pltpu.SMEM(copy_share.shape, I32),
             pltpu.SMEM(copy_source.shape, I32),
             pltpu.VMEM(route_ids.shape[::-1], I32),
             pltpu.VMEM(route_gates.shape[::-1], F32),
-            pltpu.SemaphoreType.DMA((5,)),
+            pltpu.SemaphoreType.DMA((6,)),
         ],
         compiler_params=pltpu.CompilerParams(vmem_limit_bytes=16 * MIB),
         cost_estimate=pl.CostEstimate(flops=10**8, bytes_accessed=4 * 10**6, transcendentals=0),
         name="plan",
-    )(*in_hbm(copy_share, copy_source, route_ids.T, route_gates.T, tokens))
+    )(*in_hbm(copy_share, copy_source, route_ids.T, route_gates.T, tokens, up))
 
 
 def doubler():
@@ -176,18 +196,19 @@
     return even, odd, [[held.get(i, i) for i in range(count)] for held in table]
 
 
-def shared_kernel(table, x_ref, up_hbm, down_hbm, late_hbm, *rest):
+def shared_kernel(table, x_ref, head_ref, up_hbm, down_hbm, *rest):
     outs, rest = rest[: len(table)], rest[len(table) :]
-    late_ref, up_ref, down_ref, hidden_ref, up_sem, down_sem, late_sem = rest
+    up_ref, down_ref, hidden_ref, up_sem, down_sem = rest
     rows, width = x_ref.shape
     share = outs[0].shape[0]
     hidden_width = up_ref.shape[2]
     count = chunk_count(width)
     size = width // count
     up_copies, down_copies = [], []
-    for c in range(count):
-        part = pl.ds(c * size, size)
-        up_copies.append(pltpu.make_async_copy(up_hbm.at[part], up_ref.at[part], up_sem.at[c]))
+    known = head_ref.shape[0] // size
+    for c in range(count - known):
+        there, here = pl.ds((known + c) * size, size), pl.ds(c * size, size)
+        up_copies.append(pltpu.make_async_copy(up_hbm.at[there], up_ref.at[here], up_sem.at[c]))
         up_copies[-1].start()
     for c in range(count):
         part = pl.ds(c * size, size)
@@ -195,14 +216,16 @@
             pltpu.make_async_copy(down_hbm.at[:, part], down_ref.at[:, part], down_sem.at[c])
         )
         down_copies[-1].start()
-    late = pltpu.make_async_copy(late_hbm, late_ref, late_sem)
-    late.start()
     twice = doubler()
     total = None
     for c in range(count):
         left = spread(x_ref[:, c * size : (c + 1) * size], twice)
-        up_copies[c].wait()
-        product = dot(left, up_ref.at[pl.ds(c * size, size)].reshape(2 * size, hidden_width)[...])
+        source, place = head_ref, c
+        if c >= known:
+            source, place = up_ref, c - known
+            up_copies[place].wait()
+        weights = source.at[pl.ds(place * size, size)].reshape(2 * size, hidden_width)[...]
+        product = dot(left, weights)
         total = product if total is None else total + product
     hidden_ref[...] = gated(total).astype(BF16)
     index = lax.axis_index("replica")
@@ -218,39 +241,33 @@
         result = dot(hidden, down_ref[:, c * size : (c + 1) * size]).astype(BF16)
         for number, out in enumerate(outs):
             out[:, c * size : (c + 1) * size] = result[number * share : (number + 1) * share]
-    late.wait()
-
-
-def shared(tokens, up, down, late, table):
+
+
+def shared(tokens, head, up, down, table):
     rows, width = tokens.shape
     count = chunk_count(width)
     share = rows // len(table[0])
     vmem = pl.BlockSpec(memory_space=pltpu.VMEM)
     return pl.pallas_call(
         functools.partial(shared_kernel, table),
-        out_shape=[pltpu.VMEM((share, width), BF16)] * len(table)
-        + [pltpu.VMEM(late.shape, BF16)],
-        in_specs=[vmem] + [pl.BlockSpec(memory_space=pltpu.HBM)] * 3,
-        out_specs=[vmem] * (len(table) + 1),
+        out_shape=[pltpu.VMEM((share, width), BF16)] * len(table),
+        in_specs=[vmem] * 2 + [pl.BlockSpec(memory_space=pltpu.HBM)] * 2,
+        out_specs=[vmem] * len(table),
         scratch_shapes=[
-            pltpu.VMEM(up.shape, BF16),
+            pltpu.VMEM((width - head.shape[0],) + up.shape[1:], BF16),
             pltpu.VMEM(down.shape, BF16),
             pltpu.VMEM((rows, down.shape[0]), BF16),
             pltpu.SemaphoreType.DMA((count,)),
             pltpu.SemaphoreType.DMA((count,)),
-            pltpu.SemaphoreType.DMA,
         ],
-        compiler_params=pltpu.CompilerParams(vmem_limit_bytes=24 * MIB),
+        compiler_params=pltpu.CompilerParams(vmem_limit_bytes=18 * MIB),
         cost_estimate=pl.CostEstimate(flops=3 * 10**9, bytes_accessed=25 * 10**6, transcendentals=0),
         name="shared",
-    )(tokens, *in_hbm(up, down, late))
+    )(tokens, head, *in_hbm(up, down))
 
 
 def expert_kernel(count, *refs):
-    parts, up_ref, down_hbm, outs = refs[:count], refs[count], refs[count + 1], refs[count + 2 : -2]
-    down_ref, down_sem = refs[-2:]
-    copy = pltpu.make_async_copy(down_hbm, down_ref, down_sem)
-    copy.start()
+    parts, up_ref, down_ref, outs = refs[:count], refs[count], refs[count + 1], refs[count + 2 :]
     lines, half = parts[0].shape
     hidden_width = up_ref.shape[2]
     pieces = chunk_count(half) if half % PIECE == 0 else 1
@@ -276,31 +293,26 @@
     total = totals[0] + shifted(totals[1], -slots)
     hidden = gated(total)
     hidden = jnp.where(top, hidden, shifted(hidden, slots)).astype(BF16)
-    copy.wait()
     for c in range(pieces):
         start = c * size
         first = dot(hidden, down_ref[:, start : start + size])
         second = dot(hidden, down_ref[:, half + start : half + start + size])
-        both = jnp.where(top, first, second)
-        for index in range(count):
-            outs[index][:, start : start + size] = both[index * lines : (index + 1) * lines].astype(
-                BF16
-            )
+        scatter_rows(outs, slice(start, start + size), jnp.where(top, first, second))
 
 
 def run_expert(parts, up, down):
     count = len(parts)
+    sent = bundles(count, *parts[0].shape)
     vmem = pl.BlockSpec(memory_space=pltpu.VMEM)
     return pl.pallas_call(
         functools.partial(expert_kernel, count),
-        out_shape=[jax.ShapeDtypeStruct(parts[0].shape, BF16)] * count,
-        in_specs=[vmem] * (count + 1) + [pl.BlockSpec(memory_space=pltpu.HBM)],
-        out_specs=[vmem] * count,
-        scratch_shapes=[pltpu.VMEM(down.shape, BF16), pltpu.SemaphoreType.DMA],
-        compiler_params=pltpu.CompilerParams(vmem_limit_bytes=32 * MIB),
-        cost_estimate=pl.CostEstimate(flops=6 * 10**10, bytes_accessed=13 * 10**6, transcendentals=0),
+        out_shape=sent,
+        in_specs=[vmem] * (count + 2),
+        out_specs=[vmem] * len(sent),
+        compiler_params=pltpu.CompilerParams(vmem_limit_bytes=16 * MIB),
+        cost_estimate=pl.CostEstimate(flops=10**8, bytes_accessed=13 * 10**6, transcendentals=0),
         name="routed",
-    )(*parts, up, *in_hbm(down))
+    )(*parts, up, down)
 
 
 def seat_kernel(count, capacity, source_ref, *refs):
@@ -341,7 +353,7 @@
         in_specs=[pl.BlockSpec(memory_space=pltpu.SMEM)] + [vmem] * count,
         out_specs=[vmem, vmem],
         compiler_params=pltpu.CompilerParams(vmem_limit_bytes=16 * MIB),
-        cost_estimate=pl.CostEstimate(flops=10**8, bytes_accessed=2 * 10**6, transcendentals=0),
+        cost_estimate=pl.CostEstimate(flops=10**7, bytes_accessed=10**5, transcendentals=0),
         name="seats",
     )(copy_source, *parts)
 
@@ -378,6 +390,26 @@
 def swap(array, axis, distance):
     pairs = [(i, i ^ distance) for i in range(lax.axis_size(axis))]
     return lax.ppermute(array, axis, pairs)
+
+
+def exchange(blocks, axis):
+    count = len(blocks)
+    if count == 1:
+        return blocks
+    half = count // 2
+    high = blocks[half] if half == 1 else jnp.concatenate(blocks[half:], axis=0)
+    got = jnp.split(swap(high, axis, half), half, axis=0)
+    return exchange(blocks[:half], axis) + exchange(got, axis)
+
+
+def exchange_bundles(sent, axis, then):
+    count = lax.axis_size(axis)
+    half = count // 2
+    if half == 0:
+        return list(sent)
+    got = swap(sent[half], axis, half)
+    near, got = then(exchange(list(sent[:half]), axis), got)
+    return near + exchange(jnp.split(got, half, axis=0), axis)
 
 
 def add(a, b):
@@ -402,14 +434,24 @@
     even, odd, table = line_plan(replicas)
     even_pairs = [(i, i ^ 1) for i in range(replicas)]
     odd_pairs = [(i, i + 1 if i % 2 else i - 1) for i in range(1, replicas - 1)]
-    gates, tokens, *outgoing = plan(
-        route_ids, route_gates, copy_source, copy_share, tokens, experts, capacity
+    gates, tokens, head, *outgoing = plan(
+        route_ids, route_gates, copy_source, copy_share, tokens, shared_gate_up, experts, capacity
     )
-    incoming = [outgoing[0]] + [swap(outgoing[d], "expert", d) for d in range(1, experts)]
-    *parts, up = shared(tokens, shared_gate_up, shared_down, w_gate_up[0], table)
-    got_even = got_odd = None
-
-    def phase(number, got_even, got_odd):
+    parts = shared(tokens, head, shared_gate_up, shared_down, table)
+
+    def after_shared(near, far):
+        far, _ = lax.optimization_barrier((far, parts[-1]))
+        return near, far
+
+    incoming = exchange_bundles(outgoing, "expert", after_shared)
+    sums = [None, None]
+
+    def phase(number, *after):
+        got_even, got_odd = sums
+        if got_odd is not None:
+            got_even, got_odd, *_ = lax.optimization_barrier((got_even, got_odd, *after))
+        elif got_even is not None and after:
+            got_even, *_ = lax.optimization_barrier((got_even, *after))
         send_even, send_odd = parts[even[number]], None
         if got_odd is not None:
             send_even = add(send_even, got_odd)
@@ -417,28 +459,35 @@
             send_even, got_even = lax.optimization_barrier((send_even, got_even))
         if number in odd:
             send_odd = add(parts[odd[number]], got_even)
-        got_even = lax.ppermute(send_even, "replica", even_pairs)
-        got_odd = lax.ppermute(send_odd, "replica", odd_pairs) if number in odd else None
-        return got_even, got_odd
-
-    got_even, got_odd = phase(1, None, None)
-    results = run_expert(incoming, up, w_down[0])
-    answers = [results[0]] + [swap(results[d], "expert", d) for d in range(1, experts)]
-    if replicas > 2:
-        near = min(2, experts - 1)
-        got_even, answers[near] = lax.optimization_barrier((got_even, answers[near]))
-        got_even, got_odd = phase(2, got_even, got_odd)
+        sums[0] = lax.ppermute(send_even, "replica", even_pairs)
+        sums[1] = lax.ppermute(send_odd, "replica", odd_pairs) if number in odd else None
+        return [send_even] if send_odd is None else [send_even, send_odd]
+
+    phase(1)
+    results = run_expert(incoming, w_gate_up[0], w_down[0])
+
+    def after_first(near, far):
+        if replicas > 2:
+            far, *_ = lax.optimization_barrier((far, *phase(2, near[-1])))
+        return near, far
+
+    answers = exchange_bundles(results, "expert", after_first)
     keep, send = seat_answers(answers, copy_source, capacity)
-    got = swap(send, "replica", 1)
-    for number in range(3, replicas):
-        got_even, got_odd, keep = lax.optimization_barrier((got_even, got_odd, keep))
-        got_even, got_odd = phase(number, got_even, got_odd)
-    mine = add(keep, got)
-    distance = 2
-    while distance < replicas:
-        mine = add(mine, swap(mine, "replica", distance))
+    number, distance = 3, 2
+    got, mine = swap(send, "replica", 1), keep
+    while True:
+        if number < replicas:
+            got, *_ = lax.optimization_barrier((got, *phase(number)))
+            number += 1
+        mine = add(mine, got)
+        if distance >= replicas:
+            break
+        got = swap(mine, "replica", distance)
         distance *= 2
     other = swap(mine, "replica", 1)
+    for rest in range(number, replicas):
+        phase(rest, mine)
+    got_even, got_odd = sums
     share = rows // replicas
     own_gates = lax.dynamic_slice_in_dim(gates, lax.axis_index("replica") * share, share, 0)
     if got_odd is None:

time: 71.1 us -> 66.3 us (0.932)
  Pallas kernels: 18 us -> 14.9 us
  waiting for transfers between devices: 33.1 us -> 31.4 us
    ppermute x9, waiting for transfers between devices: 30.7 us -> 20.5 us  [swap(): return lax.ppermute(array, axis, pairs)]
    ppermute x3, waiting for transfers between devices: 2.41 us -> 10.9 us  [phase(): sums[0] = lax.ppermute(send_even, 'replica', even_pairs)]
    pallas_call x1, Pallas kernels: 5.95 us -> 4.01 us  [run_expert(): pl.pallas_call(functools.partial(expert_kernel, count), out_shape=sent, i...]
    pallas_call x1, Pallas kernels: 7.78 us -> 6.1 us  [shared(): pl.pallas_call(functools.partial(shared_kernel, table), out_shape=[pltpu....]
    ppermute x3, starting transfers between devices: 10.3 us -> 9.25 us  [phase(): sums[0] = lax.ppermute(send_even, 'replica', even_pairs)]
    ppermute x9, starting transfers between devices: 7.49 us -> 8.51 us  [swap(): return lax.ppermute(array, axis, pairs)]
  transfers between devices with their start and end apart: 14 -> 14, of which waited for: 6 -> 8; matrix products, arithmetic and copies ran while one was open for 0% -> 1% of each run, Pallas kernels for 21% -> 17%
where the time goes in v2:
time: 66.3 us; the launch traced here: 66.1 us
  waiting for transfers between devices  31.4 us (47%)
  starting transfers between devices  19.1 us (29%)
  Pallas kernels  14.9 us (22%)
    ppermute x9, waiting for transfers between devices, swap(): return lax.ppermute(array, axis, pairs)  20.5 us
    ppermute x3, waiting for transfers between devices, phase(): sums[0] = lax.ppermute(send_even, 'replica', even_pairs)  10.9 us
    ppermute x3, starting transfers between devices, phase(): sums[0] = lax.ppermute(send_even, 'replica', even_pairs)  9.25 us
    ppermute x9, starting transfers between devices, swap(): return lax.ppermute(array, axis, pairs)  8.51 us
    pallas_call x1, Pallas kernels, shared(): pl.pallas_call(functools.partial(shared_kernel, table), out_shape=[pltpu....  6.1 us
    pallas_call x1, Pallas kernels, run_expert(): pl.pallas_call(functools.partial(expert_kernel, count), out_shape=sent, i...  4.01 us
    pallas_call x1, Pallas kernels, plan(): pl.pallas_call(functools.partial(plan_kernel, experts, capacity), out_sha...  2.67 us
    ppermute x2, starting transfers between devices, phase(): lax.ppermute(send_odd, 'replica', odd_pairs)  1.37 us
  transfers between devices with their start and end apart: 14, of which 8 were waited for; matrix products, arithmetic and copies ran while one was open for 1% of the time, Pallas kernels for 17%

profile of v2, /device:TPU:0, one launch (start us, length us, event | category | flops | bytes accessed | tf_op | source)
XLA Modules:
  0.0 66.1 jit_solution(10863195301993285258)
XLA Ops:
  0.0 2.7 %plan.1 = (f32[128,128]{1,0:T(8,128)S(1)}, bf16[128,7168]{1,0:T(8,128)(2,1)S(1)}, bf16[3584,2,256]{2,1,0:T(2,128)(2,1)S(1)}, bf16[24,3584]{1,0:T(8,128)(2,1)S(1)...) custom-call(s32[4]{0:T(128)} %share_hbm.1, s32[4]{0:T(128)} %source_ref.1, s32[8,128]{1,0:T(8,128)} %bitcast.8, ...), custom_call_target="tpu_custom_call" | custom-call | flops 100000000 | bytes 4000000 | tf_op jit(solution)/shard_map/plan/pallas_call | solution.py:129
  2.7 3.0 %collective-permute-start.2 = (bf16[48,3584]{1,0:T(8,128)(2,1)S(1)}, bf16[48,3584]{1,0:T(8,128)(2,1)S(1)}, u32[]{:S(2)}, u32[]{:S(2)}) collective-permute-start(bf16[48,3584]{1,0:T(8,128)(2,1)S(1)} %get-tuple-element.36), channel_id=1, source_target_pairs={{0,8},{4,12},{8,0},{12,4},{1,9},{5,13},{9,1},{13,5},{2,10},{6,14},... | collective-permute-start | bytes 1032200 | tf_op jit(solution)/shard_map/ppermute | solution.py:392
  5.7 0.0 collective-permute-start.1
  5.7 0.0 slice-start
  5.7 0.0 slice-start.1
  5.7 0.0 copy-start
  5.7 6.1 %shared.1 = (bf16[32,7168]{1,0:T(8,128)(2,1)S(1)}, bf16[32,7168]{1,0:T(8,128)(2,1)S(1)}, bf16[32,7168]{1,0:T(8,128)(2,1)S(1)}, bf16[32,7168]{1,0:T(8,128)(2,1)S(1)}) custom-call(bf16[128,7168]{1,0:T(8,128)(2,1)S(1)} %get-tuple-element.28.x_ref, bf16[3584,2,256]{2,1,0:T(2,128)(2,1)S(1)} %get-tuple-element.29.head_ref, bf16[7168,2,256]{2,1,0:T(2,128)(2,1)} %up_hbm.3, ...), custom_call_target="tpu_custom_call" | custom-call | flops 3000000000 | bytes 25000000 | tf_op jit(solution)/shard_map/shared/pallas_call | solution.py:251
  11.8 1.6 %collective-permute-start = (bf16[32,7168]{1,0:T(8,128)(2,1)S(1)}, bf16[32,7168]{1,0:T(8,128)(2,1)S(1)}, u32[]{:S(2)}, u32[]{:S(2)}) collective-permute-start(bf16[32,7168]{1,0:T(8,128)(2,1)S(1)} %get-tuple-element.33), channel_id=1, source_target_pairs={{0,1},{1,0},{2,3},{3,2},{4,5},{5,4},{6,7},{7,6},{8,9},{9,8},{10,11... | collective-permute-start | bytes 1376264 | tf_op jit(solution)/shard_map/ppermute | solution.py:462
  13.5 0.3 collective-permute-done.2
  13.8 0.1 collective-permute-start.3
  13.9 0.0 collective-permute-done.1.refs_1_
  13.9 1.4 %collective-permute-done.3.refs_3_ = bf16[24,3584]{1,0:T(8,128)(2,1)S(1)} collective-permute-done((bf16[24,3584]{1,0:T(8,128)(2,1)S(1)}, bf16[24,3584]{1,0:T(8,128)(2,1)S(1)}, u32[]{:S(2)}, u32[]{:S(2)}) %collective-permute-start.3) | collective-permute-done | bytes 172064 | tf_op jit(solution)/shard_map/ppermute | solution.py:392
  15.2 0.0 slice-done
  15.3 0.0 slice-done.1
  15.3 0.0 copy-done
  15.3 0.0 copy-start.1
  15.3 4.0 %routed.1 = (bf16[24,3584]{1,0:T(8,128)(2,1)S(1)}, bf16[24,3584]{1,0:T(8,128)(2,1)S(1)}, bf16[48,3584]{1,0:T(8,128)(2,1)S(1)}) custom-call(bf16[24,3584]{1,0:T(8,128)(2,1)S(1)} %get-tuple-element.34.refs_0_, bf16[24,3584]{1,0:T(8,128)(2,1)S(1)} %collective-permute-done.1.refs_1_, bf16[24,3584]{1,0:T(8,128)(2,1)S(1)} %get-tuple-element.54.refs_2_, ...), custom_call_target="tpu_custom_call" | custom-call | flops 100000000 | bytes 13000000 | tf_op jit(solution)/shard_map/routed/pallas_call | solution.py:307
  19.3 0.2 collective-permute-start.4
  19.5 1.7 %collective-permute-start.9 = (bf16[48,3584]{1,0:T(8,128)(2,1)S(1)}, bf16[48,3584]{1,0:T(8,128)(2,1)S(1)}, u32[]{:S(2)}, u32[]{:S(2)}) collective-permute-start(bf16[48,3584]{1,0:T(8,128)(2,1)S(1)} %get-tuple-element.46), channel_id=1, source_target_pairs={{0,8},{4,12},{8,0},{12,4},{1,9},{5,13},{9,1},{13,5},{2,10},{6,14},... | collective-permute-start | bytes 1032200 | tf_op jit(solution)/shard_map/ppermute | solution.py:392
  21.2 3.5 %collective-permute-done = bf16[32,7168]{1,0:T(8,128)(2,1)S(1)} collective-permute-done((bf16[32,7168]{1,0:T(8,128)(2,1)S(1)}, bf16[32,7168]{1,0:T(8,128)(2,1)S(1)}, u32[]{:S(2)}, u32[]{:S(2)}) %collective-permute-start) | collective-permute-done | bytes 458784 | tf_op jit(solution)/shard_map/ppermute | solution.py:462
  24.8 0.0 collective-permute-done.4.refs_1_
  24.8 0.1 add_convert_fusion.2
  24.9 0.7 %collective-permute-start.6 = (bf16[32,7168]{1,0:T(8,128)(2,1)S(1)}, bf16[32,7168]{1,0:T(8,128)(2,1)S(1)}, u32[]{:S(2)}, u32[]{:S(2)}) collective-permute-start(bf16[32,7168]{1,0:T(8,128)(2,1)S(1)} %add_convert_fusion.2), channel_id=1, source_target_pairs={{1,2},{2,1},{5,6},{6,5},{9,10},{10,9},{13,14},{14,13},{17,18},{18,... | collective-permute-start | bytes 1376264 | tf_op jit(solution)/shard_map/ppermute | solution.py:463
  25.6 4.4 %collective-permute-start.5 = (bf16[32,7168]{1,0:T(8,128)(2,1)S(1)}, bf16[32,7168]{1,0:T(8,128)(2,1)S(1)}, u32[]{:S(2)}, u32[]{:S(2)}) collective-permute-start(bf16[32,7168]{1,0:T(8,128)(2,1)S(1)} %get-tuple-element.40), channel_id=1, source_target_pairs={{0,1},{1,0},{2,3},{3,2},{4,5},{5,4},{6,7},{7,6},{8,9},{9,8},{10,11... | collective-permute-start | bytes 1376264 | tf_op jit(solution)/shard_map/ppermute | solution.py:462
  30.1 0.0 collective-permute-done.9
  30.1 0.1 collective-permute-start.10
  30.2 1.4 %collective-permute-done.10.refs_3_ = bf16[24,3584]{1,0:T(8,128)(2,1)S(1)} collective-permute-done((bf16[24,3584]{1,0:T(8,128)(2,1)S(1)}, bf16[24,3584]{1,0:T(8,128)(2,1)S(1)}, u32[]{:S(2)}, u32[]{:S(2)}) %collective-permute-start.10) | collective-permute-done | bytes 172064 | tf_op jit(solution)/shard_map/ppermute | solution.py:392
  31.6 0.0 copy-done.1
  31.6 0.9 %seats.1 = (bf16[24,3584]{1,0:T(8,128)(2,1)S(1)}, bf16[24,3584]{1,0:T(8,128)(2,1)S(1)}) custom-call(s32[4]{0:T(128)S(1)} %copy-done.1, bf16[24,3584]{1,0:T(8,128)(2,1)S(1)} %get-tuple-element.45.refs_0_, bf16[24,3584]{1,0:T(8,128)(2,1)S(1)} %collective-permute-done.4.refs_1_, bf16[24,3584]{1,0:T(8,128)(2,1)S(1)} %get-tuple-element.52.refs_2_, ...), custom_call_target="tpu_custom_call" | custom-call | flops 10000000 | bytes 100000 | tf_op jit(solution)/shard_map/seats/pallas_call | solution.py:350
  32.4 1.7 %collective-permute-start.11 = (bf16[24,3584]{1,0:T(8,128)(2,1)S(1)}, bf16[24,3584]{1,0:T(8,128)(2,1)S(1)}, u32[]{:S(2)}, u32[]{:S(2)}) collective-permute-start(bf16[24,3584]{1,0:T(8,128)(2,1)S(1)} %get-tuple-element.49), channel_id=1, source_target_pairs={{0,1},{1,0},{2,3},{3,2},{4,5},{5,4},{6,7},{7,6},{8,9},{9,8},{10,11... | collective-permute-start | bytes 516104 | tf_op jit(solution)/shard_map/ppermute | solution.py:392
  34.1 0.0 collective-permute-done.6
  34.1 7.4 %collective-permute-done.5 = bf16[32,7168]{1,0:T(8,128)(2,1)S(1)} collective-permute-done((bf16[32,7168]{1,0:T(8,128)(2,1)S(1)}, bf16[32,7168]{1,0:T(8,128)(2,1)S(1)}, u32[]{:S(2)}, u32[]{:S(2)}) %collective-permute-start.5) | collective-permute-done | bytes 458784 | tf_op jit(solution)/shard_map/ppermute | solution.py:462
  41.5 0.1 add_convert_fusion
  41.6 0.1 add_convert_fusion.1
  41.7 2.2 %collective-permute-done.11 = bf16[24,3584]{1,0:T(8,128)(2,1)S(1)} collective-permute-done((bf16[24,3584]{1,0:T(8,128)(2,1)S(1)}, bf16[24,3584]{1,0:T(8,128)(2,1)S(1)}, u32[]{:S(2)}, u32[]{:S(2)}) %collective-permute-start.11) | collective-permute-done | bytes 172064 | tf_op jit(solution)/shard_map/ppermute | solution.py:392
  43.9 1.7 %collective-permute-start.12 = (bf16[24,3584]{1,0:T(8,128)(2,1)S(1)}, bf16[24,3584]{1,0:T(8,128)(2,1)S(1)}, u32[]{:S(2)}, u32[]{:S(2)}) collective-permute-start(bf16[24,3584]{1,0:T(8,128)(2,1)S(1)} %add_convert_fusion.4), channel_id=1, source_target_pairs={{0,2},{1,3},{2,0},{3,1},{4,6},{5,7},{6,4},{7,5},{8,10},{9,11},{10,... | collective-permute-start | bytes 516104 | tf_op jit(solution)/shard_map/ppermute | solution.py:392
  45.6 0.7 %collective-permute-start.8 = (bf16[32,7168]{1,0:T(8,128)(2,1)S(1)}, bf16[32,7168]{1,0:T(8,128)(2,1)S(1)}, u32[]{:S(2)}, u32[]{:S(2)}) collective-permute-start(bf16[32,7168]{1,0:T(8,128)(2,1)S(1)} %add_convert_fusion), channel_id=1, source_target_pairs={{1,2},{2,1},{5,6},{6,5},{9,10},{10,9},{13,14},{14,13},{17,18},{18,... | collective-permute-start | bytes 1376264 | tf_op jit(solution)/shard_map/ppermute | solution.py:463
  46.3 3.2 %collective-permute-start.7 = (bf16[32,7168]{1,0:T(8,128)(2,1)S(1)}, bf16[32,7168]{1,0:T(8,128)(2,1)S(1)}, u32[]{:S(2)}, u32[]{:S(2)}) collective-permute-start(bf16[32,7168]{1,0:T(8,128)(2,1)S(1)} %add_convert_fusion.1), channel_id=1, source_target_pairs={{0,1},{1,0},{2,3},{3,2},{4,5},{5,4},{6,7},{7,6},{8,9},{9,8},{10,11... | collective-permute-start | bytes 1376264 | tf_op jit(solution)/shard_map/ppermute | solution.py:462
  49.4 5.3 %collective-permute-done.12 = bf16[24,3584]{1,0:T(8,128)(2,1)S(1)} collective-permute-done((bf16[24,3584]{1,0:T(8,128)(2,1)S(1)}, bf16[24,3584]{1,0:T(8,128)(2,1)S(1)}, u32[]{:S(2)}, u32[]{:S(2)}) %collective-permute-start.12) | collective-permute-done | bytes 172064 | tf_op jit(solution)/shard_map/ppermute | solution.py:392
  54.8 0.1 collective-permute-start.13
  54.9 9.9 %collective-permute-done.13.other_ref = bf16[24,3584]{1,0:T(8,128)(2,1)S(1)} collective-permute-done((bf16[24,3584]{1,0:T(8,128)(2,1)S(1)}, bf16[24,3584]{1,0:T(8,128)(2,1)S(1)}, u32[]{:S(2)}, u32[]{:S(2)}) %collective-permute-start.13) | collective-permute-done | bytes 172064 | tf_op jit(solution)/shard_map/ppermute | solution.py:392
  64.8 0.0 collective-permute-done.8.odd_ref
  64.8 0.0 collective-permute-done.7.even_ref
  64.8 1.3 %mix.1 = bf16[32,7168]{1,0:T(8,128)(2,1)} custom-call(bf16[32,7168]{1,0:T(8,128)(2,1)S(1)} %get-tuple-element.30.own_ref, bf16[32,7168]{1,0:T(8,128)(2,1)S(1)} %collective-permute-done.7.even_ref, bf16[32,7168]{1,0:T(8,128)(2,1)S(1)} %collective-permute-done.8.odd_ref, f32[32,128]{1,0:T(8,128)S(1)} %constant_dynamic-slice_fusion.gate_ref, ...), custom_call_target="tpu_custom_call" | custom-call | flops 100000000 | bytes 2000000 | tf_op jit(solution)/shard_map/mix/pallas_call | solution.py:379
  (6 shorter events, 0.1 us)
Async XLA Ops:
  2.7 11.1 %collective-permute-start.2 = (bf16[48,3584]{1,0:T(8,128)(2,1)S(1)}, bf16[48,3584]{1,0:T(8,128)(2,1)S(1)}, u32[]{:S(2)}, u32[]{:S(2)}) collective-permute-start(bf16[48,3584]{1,0:T(8,128)(2,1)S(1)} %get-tuple-element.36), channel_id=1, source_target_pairs={{0,8},{4,12},{8,0},{12,4},{1,9},{5,13},{9,1},{13,5},{2,10},{6,14},... | collective-permute-start | bytes 1032200 | tf_op jit(solution)/shard_map/ppermute | solution.py:392
  5.7 8.2 %collective-permute-start.1 = (bf16[24,3584]{1,0:T(8,128)(2,1)S(1)}, bf16[24,3584]{1,0:T(8,128)(2,1)S(1)}, u32[]{:S(2)}, u32[]{:S(2)}) collective-permute-start(bf16[24,3584]{1,0:T(8,128)(2,1)S(1)} %get-tuple-element.35), channel_id=1, source_target_pairs={{0,4},{4,0},{8,12},{12,8},{1,5},{5,1},{9,13},{13,9},{2,6},{6,2},{1... | collective-permute-start | bytes 516104 | tf_op jit(solution)/shard_map/ppermute | solution.py:392
  5.7 9.6 %slice-start = ((s8[7340032]{0:T(1024)(128)(4,1)}), s8[4194304]{0:T(1024)(128)(4,1)S(1)}, s32[]{:S(2)}) async-start(s8[7340032]{0:T(1024)(128)(4,1)} %bitcast.4), calls=%async_computation | async-start | bytes 8388608
  5.7 9.6 %slice-start.1 = ((s8[7340032]{0:T(1024)(128)(4,1)}), s8[3145728]{0:T(1024)(128)(4,1)S(1)}, s32[]{:S(2)}) async-start(s8[7340032]{0:T(1024)(128)(4,1)} %bitcast.4), calls=%async_computation.1 | async-start | bytes 6291456
  5.7 9.6 %copy-start = (bf16[1,256,7168]{2,1,0:T(8,128)(2,1)S(1)}, bf16[1,256,7168]{2,1,0:T(8,128)(2,1)}, u32[]{:S(2)}) copy-start(bf16[1,256,7168]{2,1,0:T(8,128)(2,1)} %param.15) | copy-start | bytes 11010052
  11.8 13.0 %collective-permute-start = (bf16[32,7168]{1,0:T(8,128)(2,1)S(1)}, bf16[32,7168]{1,0:T(8,128)(2,1)S(1)}, u32[]{:S(2)}, u32[]{:S(2)}) collective-permute-start(bf16[32,7168]{1,0:T(8,128)(2,1)S(1)} %get-tuple-element.33), channel_id=1, source_target_pairs={{0,1},{1,0},{2,3},{3,2},{4,5},{5,4},{6,7},{7,6},{8,9},{9,8},{10,11... | collective-permute-start | bytes 1376264 | tf_op jit(solution)/shard_map/ppermute | solution.py:462
  13.8 1.5 %collective-permute-start.3 = (bf16[24,3584]{1,0:T(8,128)(2,1)S(1)}, bf16[24,3584]{1,0:T(8,128)(2,1)S(1)}, u32[]{:S(2)}, u32[]{:S(2)}) collective-permute-start(bf16[24,3584]{1,0:T(8,128)(2,1)S(1)} %get-tuple-element.53), channel_id=1, source_target_pairs={{0,4},{4,0},{8,12},{12,8},{1,5},{5,1},{9,13},{13,9},{2,6},{6,2},{1... | collective-permute-start | bytes 516104 | tf_op jit(solution)/shard_map/ppermute | solution.py:392
  15.3 16.3 %copy-start.1 = (s32[4]{0:T(128)S(1)}, s32[4]{0:T(128)}, u32[]{:S(2)}) copy-start(s32[4]{0:T(128)} %source_ref.1) | copy-start | bytes 52
  19.3 5.5 %collective-permute-start.4 = (bf16[24,3584]{1,0:T(8,128)(2,1)S(1)}, bf16[24,3584]{1,0:T(8,128)(2,1)S(1)}, u32[]{:S(2)}, u32[]{:S(2)}) collective-permute-start(bf16[24,3584]{1,0:T(8,128)(2,1)S(1)} %get-tuple-element.38), channel_id=1, source_target_pairs={{0,4},{4,0},{8,12},{12,8},{1,5},{5,1},{9,13},{13,9},{2,6},{6,2},{1... | collective-permute-start | bytes 516104 | tf_op jit(solution)/shard_map/ppermute | solution.py:392
  19.5 10.6 %collective-permute-start.9 = (bf16[48,3584]{1,0:T(8,128)(2,1)S(1)}, bf16[48,3584]{1,0:T(8,128)(2,1)S(1)}, u32[]{:S(2)}, u32[]{:S(2)}) collective-permute-start(bf16[48,3584]{1,0:T(8,128)(2,1)S(1)} %get-tuple-element.46), channel_id=1, source_target_pairs={{0,8},{4,12},{8,0},{12,4},{1,9},{5,13},{9,1},{13,5},{2,10},{6,14},... | collective-permute-start | bytes 1032200 | tf_op jit(solution)/shard_map/ppermute | solution.py:392
  24.9 9.2 %collective-permute-start.6 = (bf16[32,7168]{1,0:T(8,128)(2,1)S(1)}, bf16[32,7168]{1,0:T(8,128)(2,1)S(1)}, u32[]{:S(2)}, u32[]{:S(2)}) collective-permute-start(bf16[32,7168]{1,0:T(8,128)(2,1)S(1)} %add_convert_fusion.2), channel_id=1, source_target_pairs={{1,2},{2,1},{5,6},{6,5},{9,10},{10,9},{13,14},{14,13},{17,18},{18,... | collective-permute-start | bytes 1376264 | tf_op jit(solution)/shard_map/ppermute | solution.py:463
  25.6 15.8 %collective-permute-start.5 = (bf16[32,7168]{1,0:T(8,128)(2,1)S(1)}, bf16[32,7168]{1,0:T(8,128)(2,1)S(1)}, u32[]{:S(2)}, u32[]{:S(2)}) collective-permute-start(bf16[32,7168]{1,0:T(8,128)(2,1)S(1)} %get-tuple-element.40), channel_id=1, source_target_pairs={{0,1},{1,0},{2,3},{3,2},{4,5},{5,4},{6,7},{7,6},{8,9},{9,8},{10,11... | collective-permute-start | bytes 1376264 | tf_op jit(solution)/shard_map/ppermute | solution.py:462
  30.1 1.5 %collective-permute-start.10 = (bf16[24,3584]{1,0:T(8,128)(2,1)S(1)}, bf16[24,3584]{1,0:T(8,128)(2,1)S(1)}, u32[]{:S(2)}, u32[]{:S(2)}) collective-permute-start(bf16[24,3584]{1,0:T(8,128)(2,1)S(1)} %get-tuple-element.51), channel_id=1, source_target_pairs={{0,4},{4,0},{8,12},{12,8},{1,5},{5,1},{9,13},{13,9},{2,6},{6,2},{1... | collective-permute-start | bytes 516104 | tf_op jit(solution)/shard_map/ppermute | solution.py:392
  32.4 11.4 %collective-permute-start.11 = (bf16[24,3584]{1,0:T(8,128)(2,1)S(1)}, bf16[24,3584]{1,0:T(8,128)(2,1)S(1)}, u32[]{:S(2)}, u32[]{:S(2)}) collective-permute-start(bf16[24,3584]{1,0:T(8,128)(2,1)S(1)} %get-tuple-element.49), channel_id=1, source_target_pairs={{0,1},{1,0},{2,3},{3,2},{4,5},{5,4},{6,7},{7,6},{8,9},{9,8},{10,11... | collective-permute-start | bytes 516104 | tf_op jit(solution)/shard_map/ppermute | solution.py:392
  43.9 10.8 %collective-permute-start.12 = (bf16[24,3584]{1,0:T(8,128)(2,1)S(1)}, bf16[24,3584]{1,0:T(8,128)(2,1)S(1)}, u32[]{:S(2)}, u32[]{:S(2)}) collective-permute-start(bf16[24,3584]{1,0:T(8,128)(2,1)S(1)} %add_convert_fusion.4), channel_id=1, source_target_pairs={{0,2},{1,3},{2,0},{3,1},{4,6},{5,7},{6,4},{7,5},{8,10},{9,11},{10,... | collective-permute-start | bytes 516104 | tf_op jit(solution)/shard_map/ppermute | solution.py:392
  45.6 19.2 %collective-permute-start.8 = (bf16[32,7168]{1,0:T(8,128)(2,1)S(1)}, bf16[32,7168]{1,0:T(8,128)(2,1)S(1)}, u32[]{:S(2)}, u32[]{:S(2)}) collective-permute-start(bf16[32,7168]{1,0:T(8,128)(2,1)S(1)} %add_convert_fusion), channel_id=1, source_target_pairs={{1,2},{2,1},{5,6},{6,5},{9,10},{10,9},{13,14},{14,13},{17,18},{18,... | collective-permute-start | bytes 1376264 | tf_op jit(solution)/shard_map/ppermute | solution.py:463
  46.3 18.5 %collective-permute-start.7 = (bf16[32,7168]{1,0:T(8,128)(2,1)S(1)}, bf16[32,7168]{1,0:T(8,128)(2,1)S(1)}, u32[]{:S(2)}, u32[]{:S(2)}) collective-permute-start(bf16[32,7168]{1,0:T(8,128)(2,1)S(1)} %add_convert_fusion.1), channel_id=1, source_target_pairs={{0,1},{1,0},{2,3},{3,2},{4,5},{5,4},{6,7},{7,6},{8,9},{9,8},{10,11... | collective-permute-start | bytes 1376264 | tf_op jit(solution)/shard_map/ppermute | solution.py:462
  54.8 10.0 %collective-permute-start.13 = (bf16[24,3584]{1,0:T(8,128)(2,1)S(1)}, bf16[24,3584]{1,0:T(8,128)(2,1)S(1)}, u32[]{:S(2)}, u32[]{:S(2)}) collective-permute-start(bf16[24,3584]{1,0:T(8,128)(2,1)S(1)} %add_convert_fusion.3.mine_ref), channel_id=1, source_target_pairs={{0,1},{1,0},{2,3},{3,2},{4,5},{5,4},{6,7},{7,6},{8,9},{9,8},{10,11... | collective-permute-start | bytes 516104 | tf_op jit(solution)/shard_map/ppermute | solution.py:392

commit v3 on v2

--- a/solution.py
+++ b/solution.py
@@ -358,7 +358,7 @@
     )(copy_source, *parts)
 
 
-def mix_kernel(own_ref, even_ref, odd_ref, gate_ref, mine_ref, other_ref, out_ref):
+def mix_kernel(near_ref, odd_ref, gate_ref, mine_ref, other_ref, out_ref):
     side = lax.rem(lax.axis_index("replica"), 2)
     seats, half = mine_ref.shape
     gates = gate_ref[:, :seats]
@@ -370,21 +370,21 @@
         cols = slice(position * half, (position + 1) * half)
         answers = jnp.where(side == position, mine_ref[...], other_ref[...])
         routed = dot(high, answers) + dot(middle, answers) + dot(low, answers)
-        base = own_ref[:, cols].astype(F32) + even_ref[:, cols].astype(F32) + odd_ref[:, cols].astype(F32)
+        base = near_ref[:, cols] + odd_ref[:, cols].astype(F32)
         out_ref[:, cols] = (base + routed).astype(BF16)
 
 
-def mix(own, even, odd, gates, mine, other):
+def mix(near, odd, gates, mine, other):
     vmem = pl.BlockSpec(memory_space=pltpu.VMEM)
     return pl.pallas_call(
         mix_kernel,
-        out_shape=jax.ShapeDtypeStruct(own.shape, BF16),
-        in_specs=[vmem] * 6,
+        out_shape=jax.ShapeDtypeStruct(near.shape, BF16),
+        in_specs=[vmem] * 5,
         out_specs=vmem,
         compiler_params=pltpu.CompilerParams(vmem_limit_bytes=16 * MIB),
         cost_estimate=pl.CostEstimate(flops=10**8, bytes_accessed=2 * 10**6, transcendentals=0),
         name="mix",
-    )(own, even, odd, gates, mine, other)
+    )(near, odd, gates, mine, other)
 
 
 def swap(array, axis, distance):
@@ -448,17 +448,18 @@
 
     def phase(number, *after):
         got_even, got_odd = sums
+        if got_even is not None and after:
+            got_even, *_ = lax.optimization_barrier((got_even, *after))
         if got_odd is not None:
-            got_even, got_odd, *_ = lax.optimization_barrier((got_even, got_odd, *after))
-        elif got_even is not None and after:
-            got_even, *_ = lax.optimization_barrier((got_even, *after))
+            got_odd, _ = lax.optimization_barrier((got_odd, got_even[:8, :128]))
+            got_even, got_odd = lax.optimization_barrier((got_even, got_odd))
         send_even, send_odd = parts[even[number]], None
+        if number in odd:
+            send_odd = add(parts[odd[number]], got_even)
         if got_odd is not None:
             send_even = add(send_even, got_odd)
         elif got_even is not None:
             send_even, got_even = lax.optimization_barrier((send_even, got_even))
-        if number in odd:
-            send_odd = add(parts[odd[number]], got_even)
         sums[0] = lax.ppermute(send_even, "replica", even_pairs)
         sums[1] = lax.ppermute(send_odd, "replica", odd_pairs) if number in odd else None
         return [send_even] if send_odd is None else [send_even, send_odd]
@@ -492,7 +493,9 @@
     own_gates = lax.dynamic_slice_in_dim(gates, lax.axis_index("replica") * share, share, 0)
     if got_odd is None:
         got_odd = jnp.zeros_like(got_even)
-    return mix(parts[-1], got_even, got_odd, own_gates, mine, other)
+    near = parts[-1].astype(F32) + got_even.astype(F32)
+    got_odd, near = lax.optimization_barrier((got_odd, near))
+    return mix(near, got_odd, own_gates, mine, other)
 
 
 def solution(mesh):

time: 66.3 us -> 65 us (0.980)
  starting transfers between devices: 19.1 us -> 16.2 us
  waiting for transfers between devices: 31.4 us -> 32.9 us
    ppermute x3, waiting for transfers between devices: 10.9 us -> 17.7 us  [phase(): sums[0] = lax.ppermute(send_even, 'replica', even_pairs)]
    ppermute x9, waiting for transfers between devices: 20.5 us -> 15.1 us  [swap(): return lax.ppermute(array, axis, pairs)]
    ppermute x3, starting transfers between devices: 9.25 us -> 6.37 us  [phase(): sums[0] = lax.ppermute(send_even, 'replica', even_pairs)]
  transfers between devices with their start and end apart: 14 -> 14, of which waited for: 8 -> 9; matrix products, arithmetic and copies ran while one was open for 1% -> 1% of each run, Pallas kernels for 17% -> 17%
where the time goes in v3:
time: 65 us; the launch traced here: 64.8 us
  waiting for transfers between devices  32.9 us (51%)
  starting transfers between devices  16.2 us (25%)
  Pallas kernels  14.9 us (23%)
    ppermute x3, waiting for transfers between devices, phase(): sums[0] = lax.ppermute(send_even, 'replica', even_pairs)  17.7 us
    ppermute x9, waiting for transfers between devices, swap(): return lax.ppermute(array, axis, pairs)  15.1 us
    ppermute x9, starting transfers between devices, swap(): return lax.ppermute(array, axis, pairs)  8.51 us
    ppermute x3, starting transfers between devices, phase(): sums[0] = lax.ppermute(send_even, 'replica', even_pairs)  6.37 us
    pallas_call x1, Pallas kernels, shared(): pl.pallas_call(functools.partial(shared_kernel, table), out_shape=[pltpu....  6.1 us
    pallas_call x1, Pallas kernels, run_expert(): pl.pallas_call(functools.partial(expert_kernel, count), out_shape=sent, i...  4.01 us
    pallas_call x1, Pallas kernels, plan(): pl.pallas_call(functools.partial(plan_kernel, experts, capacity), out_sha...  2.67 us
    ppermute x2, starting transfers between devices, phase(): lax.ppermute(send_odd, 'replica', odd_pairs)  1.37 us
  transfers between devices with their start and end apart: 14, of which 9 were waited for; matrix products, arithmetic and copies ran while one was open for 1% of the time, Pallas kernels for 17%

profile of v3, /device:TPU:0, one launch (start us, length us, event | category | flops | bytes accessed | tf_op | source)
XLA Modules:
  0.0 64.8 jit_solution(6799149932850050762)
XLA Ops:
  0.0 2.7 %plan.1 = (f32[128,128]{1,0:T(8,128)S(1)}, bf16[128,7168]{1,0:T(8,128)(2,1)S(1)}, bf16[3584,2,256]{2,1,0:T(2,128)(2,1)S(1)}, bf16[24,3584]{1,0:T(8,128)(2,1)S(1)...) custom-call(s32[4]{0:T(128)} %share_hbm.1, s32[4]{0:T(128)} %source_ref.1, s32[8,128]{1,0:T(8,128)} %bitcast.8, ...), custom_call_target="tpu_custom_call" | custom-call | flops 100000000 | bytes 4000000 | tf_op jit(solution)/shard_map/plan/pallas_call | solution.py:129
  2.7 3.0 %collective-permute-start.2 = (bf16[48,3584]{1,0:T(8,128)(2,1)S(1)}, bf16[48,3584]{1,0:T(8,128)(2,1)S(1)}, u32[]{:S(2)}, u32[]{:S(2)}) collective-permute-start(bf16[48,3584]{1,0:T(8,128)(2,1)S(1)} %get-tuple-element.35), channel_id=1, source_target_pairs={{0,8},{4,12},{8,0},{12,4},{1,9},{5,13},{9,1},{13,5},{2,10},{6,14},... | collective-permute-start | bytes 1032200 | tf_op jit(solution)/shard_map/ppermute | solution.py:392
  5.7 0.0 collective-permute-start.1
  5.7 0.0 slice-start
  5.7 0.0 slice-start.1
  5.7 0.0 copy-start
  5.7 6.1 %shared.1 = (bf16[32,7168]{1,0:T(8,128)(2,1)S(1)}, bf16[32,7168]{1,0:T(8,128)(2,1)S(1)}, bf16[32,7168]{1,0:T(8,128)(2,1)S(1)}, bf16[32,7168]{1,0:T(8,128)(2,1)S(1)}) custom-call(bf16[128,7168]{1,0:T(8,128)(2,1)S(1)} %get-tuple-element.29.x_ref, bf16[3584,2,256]{2,1,0:T(2,128)(2,1)S(1)} %get-tuple-element.30.head_ref, bf16[7168,2,256]{2,1,0:T(2,128)(2,1)} %up_hbm.3, ...), custom_call_target="tpu_custom_call" | custom-call | flops 3000000000 | bytes 25000000 | tf_op jit(solution)/shard_map/shared/pallas_call | solution.py:251
  11.8 1.6 %collective-permute-start = (bf16[32,7168]{1,0:T(8,128)(2,1)S(1)}, bf16[32,7168]{1,0:T(8,128)(2,1)S(1)}, u32[]{:S(2)}, u32[]{:S(2)}) collective-permute-start(bf16[32,7168]{1,0:T(8,128)(2,1)S(1)} %get-tuple-element.32), channel_id=1, source_target_pairs={{0,1},{1,0},{2,3},{3,2},{4,5},{5,4},{6,7},{7,6},{8,9},{9,8},{10,11... | collective-permute-start | bytes 1376264 | tf_op jit(solution)/shard_map/ppermute | solution.py:463
  13.5 0.3 collective-permute-done.2
  13.8 0.1 collective-permute-start.3
  13.9 0.0 collective-permute-done.1.refs_1_
  13.9 1.4 %collective-permute-done.3.refs_3_ = bf16[24,3584]{1,0:T(8,128)(2,1)S(1)} collective-permute-done((bf16[24,3584]{1,0:T(8,128)(2,1)S(1)}, bf16[24,3584]{1,0:T(8,128)(2,1)S(1)}, u32[]{:S(2)}, u32[]{:S(2)}) %collective-permute-start.3) | collective-permute-done | bytes 172064 | tf_op jit(solution)/shard_map/ppermute | solution.py:392
  15.2 0.0 slice-done
  15.3 0.0 slice-done.1
  15.3 0.0 copy-done
  15.3 0.0 copy-start.1
  15.3 4.0 %routed.1 = (bf16[24,3584]{1,0:T(8,128)(2,1)S(1)}, bf16[24,3584]{1,0:T(8,128)(2,1)S(1)}, bf16[48,3584]{1,0:T(8,128)(2,1)S(1)}) custom-call(bf16[24,3584]{1,0:T(8,128)(2,1)S(1)} %get-tuple-element.33.refs_0_, bf16[24,3584]{1,0:T(8,128)(2,1)S(1)} %collective-permute-done.1.refs_1_, bf16[24,3584]{1,0:T(8,128)(2,1)S(1)} %get-tuple-element.56.refs_2_, ...), custom_call_target="tpu_custom_call" | custom-call | flops 100000000 | bytes 13000000 | tf_op jit(solution)/shard_map/routed/pallas_call | solution.py:307
  19.3 0.2 collective-permute-start.4
  19.5 1.7 %collective-permute-start.9 = (bf16[48,3584]{1,0:T(8,128)(2,1)S(1)}, bf16[48,3584]{1,0:T(8,128)(2,1)S(1)}, u32[]{:S(2)}, u32[]{:S(2)}) collective-permute-start(bf16[48,3584]{1,0:T(8,128)(2,1)S(1)} %get-tuple-element.48), channel_id=1, source_target_pairs={{0,8},{4,12},{8,0},{12,4},{1,9},{5,13},{9,1},{13,5},{2,10},{6,14},... | collective-permute-start | bytes 1032200 | tf_op jit(solution)/shard_map/ppermute | solution.py:392
  21.2 3.5 %collective-permute-done = bf16[32,7168]{1,0:T(8,128)(2,1)S(1)} collective-permute-done((bf16[32,7168]{1,0:T(8,128)(2,1)S(1)}, bf16[32,7168]{1,0:T(8,128)(2,1)S(1)}, u32[]{:S(2)}, u32[]{:S(2)}) %collective-permute-start) | collective-permute-done | bytes 458784 | tf_op jit(solution)/shard_map/ppermute | solution.py:463
  24.8 0.0 collective-permute-done.4.refs_1_
  24.8 0.1 add_convert_fusion.2
  24.9 0.7 %collective-permute-start.6 = (bf16[32,7168]{1,0:T(8,128)(2,1)S(1)}, bf16[32,7168]{1,0:T(8,128)(2,1)S(1)}, u32[]{:S(2)}, u32[]{:S(2)}) collective-permute-start(bf16[32,7168]{1,0:T(8,128)(2,1)S(1)} %add_convert_fusion.2), channel_id=1, source_target_pairs={{1,2},{2,1},{5,6},{6,5},{9,10},{10,9},{13,14},{14,13},{17,18},{18,... | collective-permute-start | bytes 1376264 | tf_op jit(solution)/shard_map/ppermute | solution.py:464
  25.6 4.4 %collective-permute-start.5 = (bf16[32,7168]{1,0:T(8,128)(2,1)S(1)}, bf16[32,7168]{1,0:T(8,128)(2,1)S(1)}, u32[]{:S(2)}, u32[]{:S(2)}) collective-permute-start(bf16[32,7168]{1,0:T(8,128)(2,1)S(1)} %get-tuple-element.40), channel_id=1, source_target_pairs={{0,1},{1,0},{2,3},{3,2},{4,5},{5,4},{6,7},{7,6},{8,9},{9,8},{10,11... | collective-permute-start | bytes 1376264 | tf_op jit(solution)/shard_map/ppermute | solution.py:463
  30.1 0.0 collective-permute-done.9
  30.1 0.1 collective-permute-start.10
  30.2 1.4 %collective-permute-done.10.refs_3_ = bf16[24,3584]{1,0:T(8,128)(2,1)S(1)} collective-permute-done((bf16[24,3584]{1,0:T(8,128)(2,1)S(1)}, bf16[24,3584]{1,0:T(8,128)(2,1)S(1)}, u32[]{:S(2)}, u32[]{:S(2)}) %collective-permute-start.10) | collective-permute-done | bytes 172064 | tf_op jit(solution)/shard_map/ppermute | solution.py:392
  31.6 0.0 copy-done.1
  31.6 0.9 %seats.1 = (bf16[24,3584]{1,0:T(8,128)(2,1)S(1)}, bf16[24,3584]{1,0:T(8,128)(2,1)S(1)}) custom-call(s32[4]{0:T(128)S(1)} %copy-done.1, bf16[24,3584]{1,0:T(8,128)(2,1)S(1)} %get-tuple-element.47.refs_0_, bf16[24,3584]{1,0:T(8,128)(2,1)S(1)} %collective-permute-done.4.refs_1_, bf16[24,3584]{1,0:T(8,128)(2,1)S(1)} %get-tuple-element.54.refs_2_, ...), custom_call_target="tpu_custom_call" | custom-call | flops 10000000 | bytes 100000 | tf_op jit(solution)/shard_map/seats/pallas_call | solution.py:350
  32.4 1.7 %collective-permute-start.11 = (bf16[24,3584]{1,0:T(8,128)(2,1)S(1)}, bf16[24,3584]{1,0:T(8,128)(2,1)S(1)}, u32[]{:S(2)}, u32[]{:S(2)}) collective-permute-start(bf16[24,3584]{1,0:T(8,128)(2,1)S(1)} %get-tuple-element.51), channel_id=1, source_target_pairs={{0,1},{1,0},{2,3},{3,2},{4,5},{5,4},{6,7},{7,6},{8,9},{9,8},{10,11... | collective-permute-start | bytes 516104 | tf_op jit(solution)/shard_map/ppermute | solution.py:392
  34.1 0.0 collective-permute-done.6
  34.1 7.4 %collective-permute-done.5 = bf16[32,7168]{1,0:T(8,128)(2,1)S(1)} collective-permute-done((bf16[32,7168]{1,0:T(8,128)(2,1)S(1)}, bf16[32,7168]{1,0:T(8,128)(2,1)S(1)}, u32[]{:S(2)}, u32[]{:S(2)}) %collective-permute-start.5) | collective-permute-done | bytes 458784 | tf_op jit(solution)/shard_map/ppermute | solution.py:463
  41.5 0.1 add_convert_fusion.1
  41.6 0.1 add_convert_fusion
  41.7 2.2 %collective-permute-done.11 = bf16[24,3584]{1,0:T(8,128)(2,1)S(1)} collective-permute-done((bf16[24,3584]{1,0:T(8,128)(2,1)S(1)}, bf16[24,3584]{1,0:T(8,128)(2,1)S(1)}, u32[]{:S(2)}, u32[]{:S(2)}) %collective-permute-start.11) | collective-permute-done | bytes 172064 | tf_op jit(solution)/shard_map/ppermute | solution.py:392
  43.9 1.7 %collective-permute-start.12 = (bf16[24,3584]{1,0:T(8,128)(2,1)S(1)}, bf16[24,3584]{1,0:T(8,128)(2,1)S(1)}, u32[]{:S(2)}, u32[]{:S(2)}) collective-permute-start(bf16[24,3584]{1,0:T(8,128)(2,1)S(1)} %add_convert_fusion.4), channel_id=1, source_target_pairs={{0,2},{1,3},{2,0},{3,1},{4,6},{5,7},{6,4},{7,5},{8,10},{9,11},{10,... | collective-permute-start | bytes 516104 | tf_op jit(solution)/shard_map/ppermute | solution.py:392
  45.6 0.3 collective-permute-start.8
  45.9 0.7 %collective-permute-start.7 = (bf16[32,7168]{1,0:T(8,128)(2,1)S(1)}, bf16[32,7168]{1,0:T(8,128)(2,1)S(1)}, u32[]{:S(2)}, u32[]{:S(2)}) collective-permute-start(bf16[32,7168]{1,0:T(8,128)(2,1)S(1)} %add_convert_fusion.1), channel_id=1, source_target_pairs={{1,2},{2,1},{5,6},{6,5},{9,10},{10,9},{13,14},{14,13},{17,18},{18,... | collective-permute-start | bytes 1376264 | tf_op jit(solution)/shard_map/ppermute | solution.py:464
  46.6 8.1 %collective-permute-done.12 = bf16[24,3584]{1,0:T(8,128)(2,1)S(1)} collective-permute-done((bf16[24,3584]{1,0:T(8,128)(2,1)S(1)}, bf16[24,3584]{1,0:T(8,128)(2,1)S(1)}, u32[]{:S(2)}, u32[]{:S(2)}) %collective-permute-start.12) | collective-permute-done | bytes 172064 | tf_op jit(solution)/shard_map/ppermute | solution.py:392
  54.8 0.1 collective-permute-start.13
  54.8 6.8 %collective-permute-done.8 = bf16[32,7168]{1,0:T(8,128)(2,1)S(1)} collective-permute-done((bf16[32,7168]{1,0:T(8,128)(2,1)S(1)}, bf16[32,7168]{1,0:T(8,128)(2,1)S(1)}, u32[]{:S(2)}, u32[]{:S(2)}) %collective-permute-start.8) | collective-permute-done | bytes 458784 | tf_op jit(solution)/shard_map/ppermute | solution.py:463
  61.7 0.1 convert_add_fusion.near_ref
  61.8 0.0 collective-permute-done.7.odd_ref
  61.8 1.7 %collective-permute-done.13.other_ref = bf16[24,3584]{1,0:T(8,128)(2,1)S(1)} collective-permute-done((bf16[24,3584]{1,0:T(8,128)(2,1)S(1)}, bf16[24,3584]{1,0:T(8,128)(2,1)S(1)}, u32[]{:S(2)}, u32[]{:S(2)}) %collective-permute-start.13) | collective-permute-done | bytes 172064 | tf_op jit(solution)/shard_map/ppermute | solution.py:392
  63.5 1.3 %mix.1 = bf16[32,7168]{1,0:T(8,128)(2,1)} custom-call(f32[32,7168]{1,0:T(8,128)S(1)} %convert_add_fusion.near_ref, bf16[32,7168]{1,0:T(8,128)(2,1)S(1)} %collective-permute-done.7.odd_ref, f32[32,128]{1,0:T(8,128)S(1)} %constant_dynamic-slice_fusion.gate_ref, bf16[24,3584]{1,0:T(8,128)(2,1)S(1)} %add_convert_fusion.3.mine_ref, ...), custom_call_target="tpu_custom_call" | custom-call | flops 100000000 | bytes 2000000 | tf_op jit(solution)/shard_map/mix/pallas_call | solution.py:379
  (6 shorter events, 0.1 us)
Async XLA Ops:
  2.7 11.1 %collective-permute-start.2 = (bf16[48,3584]{1,0:T(8,128)(2,1)S(1)}, bf16[48,3584]{1,0:T(8,128)(2,1)S(1)}, u32[]{:S(2)}, u32[]{:S(2)}) collective-permute-start(bf16[48,3584]{1,0:T(8,128)(2,1)S(1)} %get-tuple-element.35), channel_id=1, source_target_pairs={{0,8},{4,12},{8,0},{12,4},{1,9},{5,13},{9,1},{13,5},{2,10},{6,14},... | collective-permute-start | bytes 1032200 | tf_op jit(solution)/shard_map/ppermute | solution.py:392
  5.7 8.2 %collective-permute-start.1 = (bf16[24,3584]{1,0:T(8,128)(2,1)S(1)}, bf16[24,3584]{1,0:T(8,128)(2,1)S(1)}, u32[]{:S(2)}, u32[]{:S(2)}) collective-permute-start(bf16[24,3584]{1,0:T(8,128)(2,1)S(1)} %get-tuple-element.34), channel_id=1, source_target_pairs={{0,4},{4,0},{8,12},{12,8},{1,5},{5,1},{9,13},{13,9},{2,6},{6,2},{1... | collective-permute-start | bytes 516104 | tf_op jit(solution)/shard_map/ppermute | solution.py:392
  5.7 9.6 %slice-start = ((s8[7340032]{0:T(1024)(128)(4,1)}), s8[4194304]{0:T(1024)(128)(4,1)S(1)}, s32[]{:S(2)}) async-start(s8[7340032]{0:T(1024)(128)(4,1)} %bitcast.4), calls=%async_computation | async-start | bytes 8388608
  5.7 9.6 %slice-start.1 = ((s8[7340032]{0:T(1024)(128)(4,1)}), s8[3145728]{0:T(1024)(128)(4,1)S(1)}, s32[]{:S(2)}) async-start(s8[7340032]{0:T(1024)(128)(4,1)} %bitcast.4), calls=%async_computation.1 | async-start | bytes 6291456
  5.7 9.6 %copy-start = (bf16[1,256,7168]{2,1,0:T(8,128)(2,1)S(1)}, bf16[1,256,7168]{2,1,0:T(8,128)(2,1)}, u32[]{:S(2)}) copy-start(bf16[1,256,7168]{2,1,0:T(8,128)(2,1)} %param.15) | copy-start | bytes 11010052
  11.8 13.0 %collective-permute-start = (bf16[32,7168]{1,0:T(8,128)(2,1)S(1)}, bf16[32,7168]{1,0:T(8,128)(2,1)S(1)}, u32[]{:S(2)}, u32[]{:S(2)}) collective-permute-start(bf16[32,7168]{1,0:T(8,128)(2,1)S(1)} %get-tuple-element.32), channel_id=1, source_target_pairs={{0,1},{1,0},{2,3},{3,2},{4,5},{5,4},{6,7},{7,6},{8,9},{9,8},{10,11... | collective-permute-start | bytes 1376264 | tf_op jit(solution)/shard_map/ppermute | solution.py:463
  13.8 1.5 %collective-permute-start.3 = (bf16[24,3584]{1,0:T(8,128)(2,1)S(1)}, bf16[24,3584]{1,0:T(8,128)(2,1)S(1)}, u32[]{:S(2)}, u32[]{:S(2)}) collective-permute-start(bf16[24,3584]{1,0:T(8,128)(2,1)S(1)} %get-tuple-element.55), channel_id=1, source_target_pairs={{0,4},{4,0},{8,12},{12,8},{1,5},{5,1},{9,13},{13,9},{2,6},{6,2},{1... | collective-permute-start | bytes 516104 | tf_op jit(solution)/shard_map/ppermute | solution.py:392
  15.3 16.3 %copy-start.1 = (s32[4]{0:T(128)S(1)}, s32[4]{0:T(128)}, u32[]{:S(2)}) copy-start(s32[4]{0:T(128)} %source_ref.1) | copy-start | bytes 52
  19.3 5.5 %collective-permute-start.4 = (bf16[24,3584]{1,0:T(8,128)(2,1)S(1)}, bf16[24,3584]{1,0:T(8,128)(2,1)S(1)}, u32[]{:S(2)}, u32[]{:S(2)}) collective-permute-start(bf16[24,3584]{1,0:T(8,128)(2,1)S(1)} %get-tuple-element.38), channel_id=1, source_target_pairs={{0,4},{4,0},{8,12},{12,8},{1,5},{5,1},{9,13},{13,9},{2,6},{6,2},{1... | collective-permute-start | bytes 516104 | tf_op jit(solution)/shard_map/ppermute | solution.py:392
  19.5 10.6 %collective-permute-start.9 = (bf16[48,3584]{1,0:T(8,128)(2,1)S(1)}, bf16[48,3584]{1,0:T(8,128)(2,1)S(1)}, u32[]{:S(2)}, u32[]{:S(2)}) collective-permute-start(bf16[48,3584]{1,0:T(8,128)(2,1)S(1)} %get-tuple-element.48), channel_id=1, source_target_pairs={{0,8},{4,12},{8,0},{12,4},{1,9},{5,13},{9,1},{13,5},{2,10},{6,14},... | collective-permute-start | bytes 1032200 | tf_op jit(solution)/shard_map/ppermute | solution.py:392
  24.9 9.2 %collective-permute-start.6 = (bf16[32,7168]{1,0:T(8,128)(2,1)S(1)}, bf16[32,7168]{1,0:T(8,128)(2,1)S(1)}, u32[]{:S(2)}, u32[]{:S(2)}) collective-permute-start(bf16[32,7168]{1,0:T(8,128)(2,1)S(1)} %add_convert_fusion.2), channel_id=1, source_target_pairs={{1,2},{2,1},{5,6},{6,5},{9,10},{10,9},{13,14},{14,13},{17,18},{18,... | collective-permute-start | bytes 1376264 | tf_op jit(solution)/shard_map/ppermute | solution.py:464
  25.6 15.8 %collective-permute-start.5 = (bf16[32,7168]{1,0:T(8,128)(2,1)S(1)}, bf16[32,7168]{1,0:T(8,128)(2,1)S(1)}, u32[]{:S(2)}, u32[]{:S(2)}) collective-permute-start(bf16[32,7168]{1,0:T(8,128)(2,1)S(1)} %get-tuple-element.40), channel_id=1, source_target_pairs={{0,1},{1,0},{2,3},{3,2},{4,5},{5,4},{6,7},{7,6},{8,9},{9,8},{10,11... | collective-permute-start | bytes 1376264 | tf_op jit(solution)/shard_map/ppermute | solution.py:463
  30.1 1.5 %collective-permute-start.10 = (bf16[24,3584]{1,0:T(8,128)(2,1)S(1)}, bf16[24,3584]{1,0:T(8,128)(2,1)S(1)}, u32[]{:S(2)}, u32[]{:S(2)}) collective-permute-start(bf16[24,3584]{1,0:T(8,128)(2,1)S(1)} %get-tuple-element.53), channel_id=1, source_target_pairs={{0,4},{4,0},{8,12},{12,8},{1,5},{5,1},{9,13},{13,9},{2,6},{6,2},{1... | collective-permute-start | bytes 516104 | tf_op jit(solution)/shard_map/ppermute | solution.py:392
  32.4 11.4 %collective-permute-start.11 = (bf16[24,3584]{1,0:T(8,128)(2,1)S(1)}, bf16[24,3584]{1,0:T(8,128)(2,1)S(1)}, u32[]{:S(2)}, u32[]{:S(2)}) collective-permute-start(bf16[24,3584]{1,0:T(8,128)(2,1)S(1)} %get-tuple-element.51), channel_id=1, source_target_pairs={{0,1},{1,0},{2,3},{3,2},{4,5},{5,4},{6,7},{7,6},{8,9},{9,8},{10,11... | collective-permute-start | bytes 516104 | tf_op jit(solution)/shard_map/ppermute | solution.py:392
  43.9 10.8 %collective-permute-start.12 = (bf16[24,3584]{1,0:T(8,128)(2,1)S(1)}, bf16[24,3584]{1,0:T(8,128)(2,1)S(1)}, u32[]{:S(2)}, u32[]{:S(2)}) collective-permute-start(bf16[24,3584]{1,0:T(8,128)(2,1)S(1)} %add_convert_fusion.4), channel_id=1, source_target_pairs={{0,2},{1,3},{2,0},{3,1},{4,6},{5,7},{6,4},{7,5},{8,10},{9,11},{10,... | collective-permute-start | bytes 516104 | tf_op jit(solution)/shard_map/ppermute | solution.py:392
  45.6 16.1 %collective-permute-start.8 = (bf16[32,7168]{1,0:T(8,128)(2,1)S(1)}, bf16[32,7168]{1,0:T(8,128)(2,1)S(1)}, u32[]{:S(2)}, u32[]{:S(2)}) collective-permute-start(bf16[32,7168]{1,0:T(8,128)(2,1)S(1)} %add_convert_fusion), channel_id=1, source_target_pairs={{0,1},{1,0},{2,3},{3,2},{4,5},{5,4},{6,7},{7,6},{8,9},{9,8},{10,11... | collective-permute-start | bytes 1376264 | tf_op jit(solution)/shard_map/ppermute | solution.py:463
  45.9 15.9 %collective-permute-start.7 = (bf16[32,7168]{1,0:T(8,128)(2,1)S(1)}, bf16[32,7168]{1,0:T(8,128)(2,1)S(1)}, u32[]{:S(2)}, u32[]{:S(2)}) collective-permute-start(bf16[32,7168]{1,0:T(8,128)(2,1)S(1)} %add_convert_fusion.1), channel_id=1, source_target_pairs={{1,2},{2,1},{5,6},{6,5},{9,10},{10,9},{13,14},{14,13},{17,18},{18,... | collective-permute-start | bytes 1376264 | tf_op jit(solution)/shard_map/ppermute | solution.py:464
  54.8 8.8 %collective-permute-start.13 = (bf16[24,3584]{1,0:T(8,128)(2,1)S(1)}, bf16[24,3584]{1,0:T(8,128)(2,1)S(1)}, u32[]{:S(2)}, u32[]{:S(2)}) collective-permute-start(bf16[24,3584]{1,0:T(8,128)(2,1)S(1)} %add_convert_fusion.3.mine_ref), channel_id=1, source_target_pairs={{0,1},{1,0},{2,3},{3,2},{4,5},{5,4},{6,7},{7,6},{8,9},{9,8},{10,11... | collective-permute-start | bytes 516104 | tf_op jit(solution)/shard_map/ppermute | solution.py:392

commit v4 on v3

--- a/solution.py
+++ b/solution.py
@@ -451,12 +451,16 @@
         if got_even is not None and after:
             got_even, *_ = lax.optimization_barrier((got_even, *after))
         if got_odd is not None:
-            got_odd, _ = lax.optimization_barrier((got_odd, got_even[:8, :128]))
+            held = parts[odd[number]]
+            cut = held.shape[1] // 8
+            left = add(held[:, :cut], got_even[:, :cut])
+            got_odd, left = lax.optimization_barrier((got_odd, left))
             got_even, got_odd = lax.optimization_barrier((got_even, got_odd))
         send_even, send_odd = parts[even[number]], None
         if number in odd:
             send_odd = add(parts[odd[number]], got_even)
         if got_odd is not None:
+            send_odd = jnp.concatenate([left, add(held[:, cut:], got_even[:, cut:])], axis=1)
             send_even = add(send_even, got_odd)
         elif got_even is not None:
             send_even, got_even = lax.optimization_barrier((send_even, got_even))

time: 65 us -> 62.2 us (0.957)
  waiting for transfers between devices: 32.9 us -> 30.4 us
    ppermute x3, waiting for transfers between devices: 17.7 us -> 14.9 us  [phase(): sums[0] = lax.ppermute(send_even, 'replica', even_pairs)]
    ppermute x3, starting transfers between devices: 6.37 us -> 4.85 us  [phase(): sums[0] = lax.ppermute(send_even, 'replica', even_pairs)]
    ppermute x9, starting transfers between devices: 8.51 us -> 9.73 us  [swap(): return lax.ppermute(array, axis, pairs)]
  transfers between devices with their start and end apart: 14 -> 14, of which waited for: 9 -> 10; matrix products, arithmetic and copies ran while one was open for 1% -> 1% of each run, Pallas kernels for 17% -> 18%
where the time goes in v4:
time: 62.2 us; the launch traced here: 62 us
  waiting for transfers between devices  30.4 us (49%)
  starting transfers between devices  15.9 us (26%)
  Pallas kernels  14.9 us (24%)
    ppermute x9, waiting for transfers between devices, swap(): return lax.ppermute(array, axis, pairs)  15.5 us
    ppermute x3, waiting for transfers between devices, phase(): sums[0] = lax.ppermute(send_even, 'replica', even_pairs)  14.9 us
    ppermute x9, starting transfers between devices, swap(): return lax.ppermute(array, axis, pairs)  9.73 us
    pallas_call x1, Pallas kernels, shared(): pl.pallas_call(functools.partial(shared_kernel, table), out_shape=[pltpu....  6.1 us
    ppermute x3, starting transfers between devices, phase(): sums[0] = lax.ppermute(send_even, 'replica', even_pairs)  4.85 us
    pallas_call x1, Pallas kernels, run_expert(): pl.pallas_call(functools.partial(expert_kernel, count), out_shape=sent, i...  4.01 us
    pallas_call x1, Pallas kernels, plan(): pl.pallas_call(functools.partial(plan_kernel, experts, capacity), out_sha...  2.67 us
    ppermute x2, starting transfers between devices, phase(): lax.ppermute(send_odd, 'replica', odd_pairs)  1.36 us
  transfers between devices with their start and end apart: 14, of which 10 were waited for; matrix products, arithmetic and copies ran while one was open for 1% of the time, Pallas kernels for 18%

profile of v4, /device:TPU:0, one launch (start us, length us, event | category | flops | bytes accessed | tf_op | source)
XLA Modules:
  0.0 62.0 jit_solution(15085172347042980181)
XLA Ops:
  0.0 2.7 %plan.1 = (f32[128,128]{1,0:T(8,128)S(1)}, bf16[128,7168]{1,0:T(8,128)(2,1)S(1)}, bf16[3584,2,256]{2,1,0:T(2,128)(2,1)S(1)}, bf16[24,3584]{1,0:T(8,128)(2,1)S(1)...) custom-call(s32[4]{0:T(128)} %share_hbm.1, s32[4]{0:T(128)} %source_ref.1, s32[8,128]{1,0:T(8,128)} %bitcast.8, ...), custom_call_target="tpu_custom_call" | custom-call | flops 100000000 | bytes 4000000 | tf_op jit(solution)/shard_map/plan/pallas_call | solution.py:129
  2.7 3.0 %collective-permute-start.2 = (bf16[48,3584]{1,0:T(8,128)(2,1)S(1)}, bf16[48,3584]{1,0:T(8,128)(2,1)S(1)}, u32[]{:S(2)}, u32[]{:S(2)}) collective-permute-start(bf16[48,3584]{1,0:T(8,128)(2,1)S(1)} %get-tuple-element.36), channel_id=1, source_target_pairs={{0,8},{4,12},{8,0},{12,4},{1,9},{5,13},{9,1},{13,5},{2,10},{6,14},... | collective-permute-start | bytes 1032200 | tf_op jit(solution)/shard_map/ppermute | solution.py:392
  5.7 0.0 collective-permute-start.1
  5.7 0.0 slice-start
  5.7 0.0 slice-start.1
  5.7 0.0 copy-start
  5.7 6.1 %shared.1 = (bf16[32,7168]{1,0:T(8,128)(2,1)S(1)}, bf16[32,7168]{1,0:T(8,128)(2,1)S(1)}, bf16[32,7168]{1,0:T(8,128)(2,1)S(1)}, bf16[32,7168]{1,0:T(8,128)(2,1)S(1)}) custom-call(bf16[128,7168]{1,0:T(8,128)(2,1)S(1)} %get-tuple-element.31.x_ref, bf16[3584,2,256]{2,1,0:T(2,128)(2,1)S(1)} %get-tuple-element.32.head_ref, bf16[7168,2,256]{2,1,0:T(2,128)(2,1)} %up_hbm.3, ...), custom_call_target="tpu_custom_call" | custom-call | flops 3000000000 | bytes 25000000 | tf_op jit(solution)/shard_map/shared/pallas_call | solution.py:251
  11.8 1.6 %collective-permute-start = (bf16[32,7168]{1,0:T(8,128)(2,1)S(1)}, bf16[32,7168]{1,0:T(8,128)(2,1)S(1)}, u32[]{:S(2)}, u32[]{:S(2)}) collective-permute-start(bf16[32,7168]{1,0:T(8,128)(2,1)S(1)} %get-tuple-element.33), channel_id=1, source_target_pairs={{0,1},{1,0},{2,3},{3,2},{4,5},{5,4},{6,7},{7,6},{8,9},{9,8},{10,11... | collective-permute-start | bytes 1376264 | tf_op jit(solution)/shard_map/ppermute | solution.py:467
  13.5 0.3 collective-permute-done.2
  13.8 0.1 collective-permute-start.3
  13.9 0.0 collective-permute-done.1.refs_1_
  13.9 1.4 %collective-permute-done.3.refs_3_ = bf16[24,3584]{1,0:T(8,128)(2,1)S(1)} collective-permute-done((bf16[24,3584]{1,0:T(8,128)(2,1)S(1)}, bf16[24,3584]{1,0:T(8,128)(2,1)S(1)}, u32[]{:S(2)}, u32[]{:S(2)}) %collective-permute-start.3) | collective-permute-done | bytes 172064 | tf_op jit(solution)/shard_map/ppermute | solution.py:392
  15.2 0.0 slice-done
  15.3 0.0 slice-done.1
  15.3 0.0 copy-done
  15.3 0.0 copy-start.1
  15.3 4.0 %routed.1 = (bf16[24,3584]{1,0:T(8,128)(2,1)S(1)}, bf16[24,3584]{1,0:T(8,128)(2,1)S(1)}, bf16[48,3584]{1,0:T(8,128)(2,1)S(1)}) custom-call(bf16[24,3584]{1,0:T(8,128)(2,1)S(1)} %get-tuple-element.34.refs_0_, bf16[24,3584]{1,0:T(8,128)(2,1)S(1)} %collective-permute-done.1.refs_1_, bf16[24,3584]{1,0:T(8,128)(2,1)S(1)} %get-tuple-element.60.refs_2_, ...), custom_call_target="tpu_custom_call" | custom-call | flops 100000000 | bytes 13000000 | tf_op jit(solution)/shard_map/routed/pallas_call | solution.py:307
  19.3 0.2 collective-permute-start.4
  19.5 1.7 %collective-permute-start.9 = (bf16[48,3584]{1,0:T(8,128)(2,1)S(1)}, bf16[48,3584]{1,0:T(8,128)(2,1)S(1)}, u32[]{:S(2)}, u32[]{:S(2)}) collective-permute-start(bf16[48,3584]{1,0:T(8,128)(2,1)S(1)} %get-tuple-element.52), channel_id=1, source_target_pairs={{0,8},{4,12},{8,0},{12,4},{1,9},{5,13},{9,1},{13,5},{2,10},{6,14},... | collective-permute-start | bytes 1032200 | tf_op jit(solution)/shard_map/ppermute | solution.py:392
  21.2 3.5 %collective-permute-done = bf16[32,7168]{1,0:T(8,128)(2,1)S(1)} collective-permute-done((bf16[32,7168]{1,0:T(8,128)(2,1)S(1)}, bf16[32,7168]{1,0:T(8,128)(2,1)S(1)}, u32[]{:S(2)}, u32[]{:S(2)}) %collective-permute-start) | collective-permute-done | bytes 458784 | tf_op jit(solution)/shard_map/ppermute | solution.py:467
  24.8 0.0 collective-permute-done.4.refs_1_
  24.8 0.1 add_convert_fusion.1
  24.9 1.6 %collective-permute-start.6 = (bf16[32,7168]{1,0:T(8,128)(2,1)S(1)}, bf16[32,7168]{1,0:T(8,128)(2,1)S(1)}, u32[]{:S(2)}, u32[]{:S(2)}) collective-permute-start(bf16[32,7168]{1,0:T(8,128)(2,1)S(1)} %get-tuple-element.42), channel_id=1, source_target_pairs={{0,1},{1,0},{2,3},{3,2},{4,5},{5,4},{6,7},{7,6},{8,9},{9,8},{10,11... | collective-permute-start | bytes 1376264 | tf_op jit(solution)/shard_map/ppermute | solution.py:467
  26.6 0.7 %collective-permute-start.5 = (bf16[32,7168]{1,0:T(8,128)(2,1)S(1)}, bf16[32,7168]{1,0:T(8,128)(2,1)S(1)}, u32[]{:S(2)}, u32[]{:S(2)}) collective-permute-start(bf16[32,7168]{1,0:T(8,128)(2,1)S(1)} %add_convert_fusion.1), channel_id=1, source_target_pairs={{1,2},{2,1},{5,6},{6,5},{9,10},{10,9},{13,14},{14,13},{17,18},{18,... | collective-permute-start | bytes 1376264 | tf_op jit(solution)/shard_map/ppermute | solution.py:468
  27.2 2.6 %collective-permute-done.9 = bf16[48,3584]{1,0:T(8,128)(2,1)S(1)} collective-permute-done((bf16[48,3584]{1,0:T(8,128)(2,1)S(1)}, bf16[48,3584]{1,0:T(8,128)(2,1)S(1)}, u32[]{:S(2)}, u32[]{:S(2)}) %collective-permute-start.9) | collective-permute-done | bytes 344096 | tf_op jit(solution)/shard_map/ppermute | solution.py:392
  29.9 0.1 collective-permute-start.10
  29.9 1.4 %collective-permute-done.10.refs_3_ = bf16[24,3584]{1,0:T(8,128)(2,1)S(1)} collective-permute-done((bf16[24,3584]{1,0:T(8,128)(2,1)S(1)}, bf16[24,3584]{1,0:T(8,128)(2,1)S(1)}, u32[]{:S(2)}, u32[]{:S(2)}) %collective-permute-start.10) | collective-permute-done | bytes 172064 | tf_op jit(solution)/shard_map/ppermute | solution.py:392
  31.3 0.0 copy-done.1
  31.3 0.9 %seats.1 = (bf16[24,3584]{1,0:T(8,128)(2,1)S(1)}, bf16[24,3584]{1,0:T(8,128)(2,1)S(1)}) custom-call(s32[4]{0:T(128)S(1)} %copy-done.1, bf16[24,3584]{1,0:T(8,128)(2,1)S(1)} %get-tuple-element.51.refs_0_, bf16[24,3584]{1,0:T(8,128)(2,1)S(1)} %collective-permute-done.4.refs_1_, bf16[24,3584]{1,0:T(8,128)(2,1)S(1)} %get-tuple-element.58.refs_2_, ...), custom_call_target="tpu_custom_call" | custom-call | flops 10000000 | bytes 100000 | tf_op jit(solution)/shard_map/seats/pallas_call | solution.py:350
  32.2 1.9 %collective-permute-start.11 = (bf16[24,3584]{1,0:T(8,128)(2,1)S(1)}, bf16[24,3584]{1,0:T(8,128)(2,1)S(1)}, u32[]{:S(2)}, u32[]{:S(2)}) collective-permute-start(bf16[24,3584]{1,0:T(8,128)(2,1)S(1)} %get-tuple-element.55), channel_id=1, source_target_pairs={{0,1},{1,0},{2,3},{3,2},{4,5},{5,4},{6,7},{7,6},{8,9},{9,8},{10,11... | collective-permute-start | bytes 516104 | tf_op jit(solution)/shard_map/ppermute | solution.py:392
  34.1 4.3 %collective-permute-done.6 = bf16[32,7168]{1,0:T(8,128)(2,1)S(1)} collective-permute-done((bf16[32,7168]{1,0:T(8,128)(2,1)S(1)}, bf16[32,7168]{1,0:T(8,128)(2,1)S(1)}, u32[]{:S(2)}, u32[]{:S(2)}) %collective-permute-start.6) | collective-permute-done | bytes 458784 | tf_op jit(solution)/shard_map/ppermute | solution.py:467
  38.4 0.0 collective-permute-done.5
  38.4 0.1 add_convert_fusion.2
  38.5 0.1 add_convert_fusion
  38.7 2.1 %collective-permute-done.11 = bf16[24,3584]{1,0:T(8,128)(2,1)S(1)} collective-permute-done((bf16[24,3584]{1,0:T(8,128)(2,1)S(1)}, bf16[24,3584]{1,0:T(8,128)(2,1)S(1)}, u32[]{:S(2)}, u32[]{:S(2)}) %collective-permute-start.11) | collective-permute-done | bytes 172064 | tf_op jit(solution)/shard_map/ppermute | solution.py:392
  40.8 2.7 %collective-permute-start.12 = (bf16[24,3584]{1,0:T(8,128)(2,1)S(1)}, bf16[24,3584]{1,0:T(8,128)(2,1)S(1)}, u32[]{:S(2)}, u32[]{:S(2)}) collective-permute-start(bf16[24,3584]{1,0:T(8,128)(2,1)S(1)} %add_convert_fusion.4), channel_id=1, source_target_pairs={{0,2},{1,3},{2,0},{3,1},{4,6},{5,7},{6,4},{7,5},{8,10},{9,11},{10,... | collective-permute-start | bytes 516104 | tf_op jit(solution)/shard_map/ppermute | solution.py:392
  43.5 1.6 %collective-permute-start.8 = (bf16[32,7168]{1,0:T(8,128)(2,1)S(1)}, bf16[32,7168]{1,0:T(8,128)(2,1)S(1)}, u32[]{:S(2)}, u32[]{:S(2)}) collective-permute-start(bf16[32,7168]{1,0:T(8,128)(2,1)S(1)} %add_convert_fusion), channel_id=1, source_target_pairs={{0,1},{1,0},{2,3},{3,2},{4,5},{5,4},{6,7},{7,6},{8,9},{9,8},{10,11... | collective-permute-start | bytes 1376264 | tf_op jit(solution)/shard_map/ppermute | solution.py:467
  45.1 0.7 %collective-permute-start.7 = (bf16[32,7168]{1,0:T(8,128)(2,1)S(1)}, bf16[32,7168]{1,0:T(8,128)(2,1)S(1)}, u32[]{:S(2)}, u32[]{:S(2)}) collective-permute-start(bf16[32,7168]{1,0:T(8,128)(2,1)S(1)} %pad_maximum_fusion), channel_id=1, source_target_pairs={{1,2},{2,1},{5,6},{6,5},{9,10},{10,9},{13,14},{14,13},{17,18},{18,... | collective-permute-start | bytes 1376264 | tf_op jit(solution)/shard_map/ppermute | solution.py:468
  45.8 6.0 %collective-permute-done.12 = bf16[24,3584]{1,0:T(8,128)(2,1)S(1)} collective-permute-done((bf16[24,3584]{1,0:T(8,128)(2,1)S(1)}, bf16[24,3584]{1,0:T(8,128)(2,1)S(1)}, u32[]{:S(2)}, u32[]{:S(2)}) %collective-permute-start.12) | collective-permute-done | bytes 172064 | tf_op jit(solution)/shard_map/ppermute | solution.py:392
  51.8 0.1 collective-permute-start.13
  51.9 7.0 %collective-permute-done.8 = bf16[32,7168]{1,0:T(8,128)(2,1)S(1)} collective-permute-done((bf16[32,7168]{1,0:T(8,128)(2,1)S(1)}, bf16[32,7168]{1,0:T(8,128)(2,1)S(1)}, u32[]{:S(2)}, u32[]{:S(2)}) %collective-permute-start.8) | collective-permute-done | bytes 458784 | tf_op jit(solution)/shard_map/ppermute | solution.py:467
  58.9 0.1 convert_add_fusion.near_ref
  59.0 0.0 collective-permute-done.7.odd_ref
  59.0 1.7 %collective-permute-done.13.other_ref = bf16[24,3584]{1,0:T(8,128)(2,1)S(1)} collective-permute-done((bf16[24,3584]{1,0:T(8,128)(2,1)S(1)}, bf16[24,3584]{1,0:T(8,128)(2,1)S(1)}, u32[]{:S(2)}, u32[]{:S(2)}) %collective-permute-start.13) | collective-permute-done | bytes 172064 | tf_op jit(solution)/shard_map/ppermute | solution.py:392
  60.8 1.3 %mix.1 = bf16[32,7168]{1,0:T(8,128)(2,1)} custom-call(f32[32,7168]{1,0:T(8,128)S(1)} %convert_add_fusion.near_ref, bf16[32,7168]{1,0:T(8,128)(2,1)S(1)} %collective-permute-done.7.odd_ref, f32[32,128]{1,0:T(8,128)S(1)} %constant_dynamic-slice_fusion.gate_ref, bf16[24,3584]{1,0:T(8,128)(2,1)S(1)} %add_convert_fusion.3.mine_ref, ...), custom_call_target="tpu_custom_call" | custom-call | flops 100000000 | bytes 2000000 | tf_op jit(solution)/shard_map/mix/pallas_call | solution.py:379
  (8 shorter events, 0.2 us)
Async XLA Ops:
  2.7 11.1 %collective-permute-start.2 = (bf16[48,3584]{1,0:T(8,128)(2,1)S(1)}, bf16[48,3584]{1,0:T(8,128)(2,1)S(1)}, u32[]{:S(2)}, u32[]{:S(2)}) collective-permute-start(bf16[48,3584]{1,0:T(8,128)(2,1)S(1)} %get-tuple-element.36), channel_id=1, source_target_pairs={{0,8},{4,12},{8,0},{12,4},{1,9},{5,13},{9,1},{13,5},{2,10},{6,14},... | collective-permute-start | bytes 1032200 | tf_op jit(solution)/shard_map/ppermute | solution.py:392
  5.7 8.2 %collective-permute-start.1 = (bf16[24,3584]{1,0:T(8,128)(2,1)S(1)}, bf16[24,3584]{1,0:T(8,128)(2,1)S(1)}, u32[]{:S(2)}, u32[]{:S(2)}) collective-permute-start(bf16[24,3584]{1,0:T(8,128)(2,1)S(1)} %get-tuple-element.35), channel_id=1, source_target_pairs={{0,4},{4,0},{8,12},{12,8},{1,5},{5,1},{9,13},{13,9},{2,6},{6,2},{1... | collective-permute-start | bytes 516104 | tf_op jit(solution)/shard_map/ppermute | solution.py:392
  5.7 9.6 %slice-start = ((s8[7340032]{0:T(1024)(128)(4,1)}), s8[4194304]{0:T(1024)(128)(4,1)S(1)}, s32[]{:S(2)}) async-start(s8[7340032]{0:T(1024)(128)(4,1)} %bitcast.4), calls=%async_computation | async-start | bytes 8388608
  5.7 9.6 %slice-start.1 = ((s8[7340032]{0:T(1024)(128)(4,1)}), s8[3145728]{0:T(1024)(128)(4,1)S(1)}, s32[]{:S(2)}) async-start(s8[7340032]{0:T(1024)(128)(4,1)} %bitcast.4), calls=%async_computation.1 | async-start | bytes 6291456
  5.7 9.6 %copy-start = (bf16[1,256,7168]{2,1,0:T(8,128)(2,1)S(1)}, bf16[1,256,7168]{2,1,0:T(8,128)(2,1)}, u32[]{:S(2)}) copy-start(bf16[1,256,7168]{2,1,0:T(8,128)(2,1)} %param.15) | copy-start | bytes 11010052
  11.8 13.0 %collective-permute-start = (bf16[32,7168]{1,0:T(8,128)(2,1)S(1)}, bf16[32,7168]{1,0:T(8,128)(2,1)S(1)}, u32[]{:S(2)}, u32[]{:S(2)}) collective-permute-start(bf16[32,7168]{1,0:T(8,128)(2,1)S(1)} %get-tuple-element.33), channel_id=1, source_target_pairs={{0,1},{1,0},{2,3},{3,2},{4,5},{5,4},{6,7},{7,6},{8,9},{9,8},{10,11... | collective-permute-start | bytes 1376264 | tf_op jit(solution)/shard_map/ppermute | solution.py:467
  13.8 1.5 %collective-permute-start.3 = (bf16[24,3584]{1,0:T(8,128)(2,1)S(1)}, bf16[24,3584]{1,0:T(8,128)(2,1)S(1)}, u32[]{:S(2)}, u32[]{:S(2)}) collective-permute-start(bf16[24,3584]{1,0:T(8,128)(2,1)S(1)} %get-tuple-element.59), channel_id=1, source_target_pairs={{0,4},{4,0},{8,12},{12,8},{1,5},{5,1},{9,13},{13,9},{2,6},{6,2},{1... | collective-permute-start | bytes 516104 | tf_op jit(solution)/shard_map/ppermute | solution.py:392
  15.3 16.1 %copy-start.1 = (s32[4]{0:T(128)S(1)}, s32[4]{0:T(128)}, u32[]{:S(2)}) copy-start(s32[4]{0:T(128)} %source_ref.1) | copy-start | bytes 52
  19.3 5.5 %collective-permute-start.4 = (bf16[24,3584]{1,0:T(8,128)(2,1)S(1)}, bf16[24,3584]{1,0:T(8,128)(2,1)S(1)}, u32[]{:S(2)}, u32[]{:S(2)}) collective-permute-start(bf16[24,3584]{1,0:T(8,128)(2,1)S(1)} %get-tuple-element.39), channel_id=1, source_target_pairs={{0,4},{4,0},{8,12},{12,8},{1,5},{5,1},{9,13},{13,9},{2,6},{6,2},{1... | collective-permute-start | bytes 516104 | tf_op jit(solution)/shard_map/ppermute | solution.py:392
  19.5 10.3 %collective-permute-start.9 = (bf16[48,3584]{1,0:T(8,128)(2,1)S(1)}, bf16[48,3584]{1,0:T(8,128)(2,1)S(1)}, u32[]{:S(2)}, u32[]{:S(2)}) collective-permute-start(bf16[48,3584]{1,0:T(8,128)(2,1)S(1)} %get-tuple-element.52), channel_id=1, source_target_pairs={{0,8},{4,12},{8,0},{12,4},{1,9},{5,13},{9,1},{13,5},{2,10},{6,14},... | collective-permute-start | bytes 1032200 | tf_op jit(solution)/shard_map/ppermute | solution.py:392
  24.9 13.5 %collective-permute-start.6 = (bf16[32,7168]{1,0:T(8,128)(2,1)S(1)}, bf16[32,7168]{1,0:T(8,128)(2,1)S(1)}, u32[]{:S(2)}, u32[]{:S(2)}) collective-permute-start(bf16[32,7168]{1,0:T(8,128)(2,1)S(1)} %get-tuple-element.42), channel_id=1, source_target_pairs={{0,1},{1,0},{2,3},{3,2},{4,5},{5,4},{6,7},{7,6},{8,9},{9,8},{10,11... | collective-permute-start | bytes 1376264 | tf_op jit(solution)/shard_map/ppermute | solution.py:467
  26.6 11.9 %collective-permute-start.5 = (bf16[32,7168]{1,0:T(8,128)(2,1)S(1)}, bf16[32,7168]{1,0:T(8,128)(2,1)S(1)}, u32[]{:S(2)}, u32[]{:S(2)}) collective-permute-start(bf16[32,7168]{1,0:T(8,128)(2,1)S(1)} %add_convert_fusion.1), channel_id=1, source_target_pairs={{1,2},{2,1},{5,6},{6,5},{9,10},{10,9},{13,14},{14,13},{17,18},{18,... | collective-permute-start | bytes 1376264 | tf_op jit(solution)/shard_map/ppermute | solution.py:468
  29.9 1.5 %collective-permute-start.10 = (bf16[24,3584]{1,0:T(8,128)(2,1)S(1)}, bf16[24,3584]{1,0:T(8,128)(2,1)S(1)}, u32[]{:S(2)}, u32[]{:S(2)}) collective-permute-start(bf16[24,3584]{1,0:T(8,128)(2,1)S(1)} %get-tuple-element.57), channel_id=1, source_target_pairs={{0,4},{4,0},{8,12},{12,8},{1,5},{5,1},{9,13},{13,9},{2,6},{6,2},{1... | collective-permute-start | bytes 516104 | tf_op jit(solution)/shard_map/ppermute | solution.py:392
  32.2 8.6 %collective-permute-start.11 = (bf16[24,3584]{1,0:T(8,128)(2,1)S(1)}, bf16[24,3584]{1,0:T(8,128)(2,1)S(1)}, u32[]{:S(2)}, u32[]{:S(2)}) collective-permute-start(bf16[24,3584]{1,0:T(8,128)(2,1)S(1)} %get-tuple-element.55), channel_id=1, source_target_pairs={{0,1},{1,0},{2,3},{3,2},{4,5},{5,4},{6,7},{7,6},{8,9},{9,8},{10,11... | collective-permute-start | bytes 516104 | tf_op jit(solution)/shard_map/ppermute | solution.py:392
  40.8 10.9 %collective-permute-start.12 = (bf16[24,3584]{1,0:T(8,128)(2,1)S(1)}, bf16[24,3584]{1,0:T(8,128)(2,1)S(1)}, u32[]{:S(2)}, u32[]{:S(2)}) collective-permute-start(bf16[24,3584]{1,0:T(8,128)(2,1)S(1)} %add_convert_fusion.4), channel_id=1, source_target_pairs={{0,2},{1,3},{2,0},{3,1},{4,6},{5,7},{6,4},{7,5},{8,10},{9,11},{10,... | collective-permute-start | bytes 516104 | tf_op jit(solution)/shard_map/ppermute | solution.py:392
  43.5 15.4 %collective-permute-start.8 = (bf16[32,7168]{1,0:T(8,128)(2,1)S(1)}, bf16[32,7168]{1,0:T(8,128)(2,1)S(1)}, u32[]{:S(2)}, u32[]{:S(2)}) collective-permute-start(bf16[32,7168]{1,0:T(8,128)(2,1)S(1)} %add_convert_fusion), channel_id=1, source_target_pairs={{0,1},{1,0},{2,3},{3,2},{4,5},{5,4},{6,7},{7,6},{8,9},{9,8},{10,11... | collective-permute-start | bytes 1376264 | tf_op jit(solution)/shard_map/ppermute | solution.py:467
  45.1 13.9 %collective-permute-start.7 = (bf16[32,7168]{1,0:T(8,128)(2,1)S(1)}, bf16[32,7168]{1,0:T(8,128)(2,1)S(1)}, u32[]{:S(2)}, u32[]{:S(2)}) collective-permute-start(bf16[32,7168]{1,0:T(8,128)(2,1)S(1)} %pad_maximum_fusion), channel_id=1, source_target_pairs={{1,2},{2,1},{5,6},{6,5},{9,10},{10,9},{13,14},{14,13},{17,18},{18,... | collective-permute-start | bytes 1376264 | tf_op jit(solution)/shard_map/ppermute | solution.py:468
  51.8 8.9 %collective-permute-start.13 = (bf16[24,3584]{1,0:T(8,128)(2,1)S(1)}, bf16[24,3584]{1,0:T(8,128)(2,1)S(1)}, u32[]{:S(2)}, u32[]{:S(2)}) collective-permute-start(bf16[24,3584]{1,0:T(8,128)(2,1)S(1)} %add_convert_fusion.3.mine_ref), channel_id=1, source_target_pairs={{0,1},{1,0},{2,3},{3,2},{4,5},{5,4},{6,7},{7,6},{8,9},{9,8},{10,11... | collective-permute-start | bytes 516104 | tf_op jit(solution)/shard_map/ppermute | solution.py:392
